TPU v7x, 512 devices: a whole 4x4x16 slice. The times are simulated.
512 devices in a mesh: space: 32 (over y, z_lo, core), date: 16 (over x, z_hi).
Axes of the slice: x: 4, y: 4, z: 16 (z_hi: 4, z_lo: 4; z = z_hi * 4 + z_lo), core: 2. Of those that a mesh axis runs over, the one named last changes fastest.
Arguments:
- hr_qkv: bfloat16 [3, 16, 256, 16, 2816], P(None, 'date', 'space'), may hold values from -70 to 70
- s_qkv: bfloat16 [3, 16, 256, 16, 1024], P(None, 'date', 'space'), may hold values from -70 to 70
- hr_proj: bfloat16 [2816, 2816], P(None, 'date'), may hold values from -0.109375 to 0.109375
- s_proj: bfloat16 [1024, 1024], P('date'), may hold values from -0.1875 to 0.1875
- shifts: int32 [16], P('date'), may hold values from 0 to 4
- cloud_valid: int32 [16, 256, 16], P(None, 'space', 'date'), may hold values 0 or 1
- date_embed: bfloat16 [16, 3840], replicated, may hold values from -16 to 16
- norm_gain: float32 [3840], replicated, may hold values from 0.1 to 1.9
Outputs:
- merged_out: bfloat16 [16, 256, 16, 3840], P(None, 'space', 'date')
All inputs are finite; a program needn't handle non-finite values. No bound on the sum of `cloud_valid` on one device may be relied on, other than what follows from the above.
Results may differ from a plain program's by a relative error of at most 0.008.
Values may be sent and summed in bfloat16 or wider, within the bound.
No kernel may reach another device: no remote copies, remote signals or barrier semaphores. Data moves between devices by JAX's collectives and lax.ppermute only.
A program may use at most 128 MiB of HBM per device.

v0:
```python
import jax
import jax.numpy as jnp
from jax import lax
from jax.sharding import PartitionSpec as P

HRW = 2816
SW = 1024
HR_HEAD = 32
S_HEAD = 64
T_HEAD = 64
WIN = 8


def passed_along(x, axis, by):
    size = lax.axis_size(axis)
    return lax.ppermute(x, axis, [(i, (i + by) % size) for i in range(size)])


def attend(queries, key_part, value_part, head_dim):
    scores = jnp.einsum("nqhd,nkhd->nhqk", queries, key_part, preferred_element_type=jnp.float32)
    scores = scores * (1.0 / head_dim**0.5)
    scores = scores - jnp.max(scores, axis=-1, keepdims=True)
    expo = jnp.exp(scores)
    weights = (expo / jnp.sum(expo, axis=-1, keepdims=True)).astype(jnp.bfloat16)
    mixed = jnp.einsum("nhqk,nkhd->nqhd", weights, value_part, preferred_element_type=jnp.float32)
    return mixed.astype(jnp.bfloat16).reshape(mixed.shape[0], mixed.shape[1], -1)


def window_attention(queries, key_part, value_part, head_dim):
    row_count, col_count, width = queries.shape

    def split(tensor):
        tensor = tensor.reshape(
            row_count // WIN, WIN, col_count // WIN, WIN, width // head_dim, head_dim
        )
        return tensor.transpose(0, 2, 1, 3, 4, 5).reshape(
            -1, WIN * WIN, width // head_dim, head_dim
        )

    mixed = attend(split(queries), split(key_part), split(value_part), head_dim)
    mixed = mixed.reshape(row_count // WIN, col_count // WIN, WIN, WIN, width).transpose(
        0, 2, 1, 3, 4
    )
    return mixed.reshape(row_count, col_count, width)


def add_slice(source, piece):
    return jnp.dot(source, piece, preferred_element_type=jnp.float32)


def temporal(merged, valid, date_embed, norm_gain):
    date_count, patch_count, channels = merged.shape
    joined = (merged.astype(jnp.float32) + date_embed.astype(jnp.float32)[:, None, :]).astype(
        jnp.bfloat16
    )
    heads = joined.reshape(date_count, patch_count, channels // T_HEAD, T_HEAD)
    scores = jnp.einsum("tphd,sphd->phts", heads, heads, preferred_element_type=jnp.float32) * (
        1.0 / T_HEAD
    )
    same = lax.broadcasted_iota(jnp.int32, (date_count, date_count), 0) == lax.broadcasted_iota(
        jnp.int32, (date_count, date_count), 1
    )
    keep = (valid.T[:, None, None, :] > 0) | same[None, None]
    scores = jnp.where(keep, scores, jnp.float32(-1e30))
    scores = scores - jnp.max(scores, axis=-1, keepdims=True)
    expo = jnp.where(keep, jnp.exp(scores), jnp.float32(0.0))
    weights = (expo / jnp.sum(expo, axis=-1, keepdims=True)).astype(jnp.bfloat16)
    mixed_heads = jnp.einsum("phts,sphd->tphd", weights, heads, preferred_element_type=jnp.float32)
    mixed = joined.astype(jnp.float32) + mixed_heads.reshape(date_count, patch_count, channels)
    scale = lax.rsqrt(jnp.mean(mixed * mixed, axis=-1, keepdims=True) + 1e-06)
    return (mixed * scale * norm_gain).astype(jnp.bfloat16)


def per_device(hr_qkv, s_qkv, hr_proj, s_proj, shifts, cloud_valid, date_embed, norm_gain):
    margin = WIN // 2
    offset = shifts[0]
    row_count = hr_qkv.shape[2]
    col_count = hr_qkv.shape[3]
    below = passed_along(hr_qkv[:, :, :margin], "space", -1)
    stacked = jnp.concatenate([hr_qkv[:, 0], below[:, 0]], axis=1)
    taken = lax.dynamic_slice_in_dim(stacked, offset, row_count, 1)
    taken = jnp.roll(taken, -offset, axis=2)
    window_out = window_attention(taken[0], taken[1], taken[2], HR_HEAD)
    above = passed_along(window_out[row_count - margin :], "space", 1)
    window_out = lax.dynamic_slice_in_dim(
        jnp.concatenate([above, window_out], axis=0), margin - offset, row_count, 0
    )
    window_out = jnp.roll(window_out, offset, axis=1)
    hr_flat = window_out.reshape(-1, HRW)
    tiles = s_qkv[:, 0].reshape(3, 1, row_count * col_count, SW // S_HEAD, S_HEAD)
    tile_out = attend(tiles[0], tiles[1], tiles[2], S_HEAD).reshape(-1, SW)
    s_out = add_slice(tile_out, lax.all_gather(s_proj, "date", axis=0, tiled=True))
    s_out = s_out.astype(jnp.bfloat16).reshape(1, row_count, col_count, SW)
    hr_part = jnp.einsum(
        "kph,hc->kpc",
        lax.all_gather(hr_flat[None], "date", axis=0, tiled=True),
        hr_proj,
        preferred_element_type=jnp.float32,
    ).astype(jnp.bfloat16)
    hr_part = hr_part.reshape(hr_part.shape[0], row_count, col_count, hr_proj.shape[1])
    hr_moved = lax.all_to_all(hr_part, "date", split_axis=2, concat_axis=3, tiled=True)
    s_moved = lax.all_to_all(s_out, "date", split_axis=2, concat_axis=0, tiled=True)
    merged = jnp.concatenate([hr_moved, s_moved], axis=-1)
    date_count, own_rows, own_cols, channels = merged.shape
    result = temporal(
        merged.reshape(date_count, own_rows * own_cols, channels),
        cloud_valid.reshape(date_count, -1),
        date_embed,
        norm_gain,
    )
    return result.reshape(date_count, own_rows, own_cols, channels)


def solution(mesh):
    in_specs = (
        P(None, "date", "space", None, None),
        P(None, "date", "space", None, None),
        P(None, "date"),
        P("date", None),
        P("date"),
        P(None, "space", "date"),
        P(),
        P(),
    )
    out_specs = P(None, "space", "date", None)
    return jax.shard_map(
        per_device, mesh=mesh, in_specs=in_specs, out_specs=out_specs, check_vma=False
    )
```

profile of v0, /device:TPU:41, one launch (start us, length us, event | category | flops | bytes accessed | tf_op | source)
XLA Modules:
  0.0 617.4 jit_solution(6657248135853867390)
XLA Ops:
  6.5 0.0 all-gather.3.cloned.1.call-start
  6.5 2.4 slice.30
  9.0 2.6 collective-permute-start
  12.2 14.0 %collective-permute-done = bf16[3,1,4,16,2816]{4,3,2,1,0:T(8,128)(2,1)} collective-permute-done((bf16[3,1,4,16,2816]{4,3,2,1,0:T(8,128)(2,1)}, bf16[3,1,4,16,2816]{4,3,2,1,0:T(8,128)(2,1)}, u32[]{:S(2)}, u32[]{:S(2)}) %collective-permute-start) | collective-permute-done | bytes 1081376 | tf_op jit(solution)/shard_map/ppermute | solution.py:16
  26.2 1.9 fusion.9
  28.1 1.6 fusion.10
  29.7 0.1 fusion.41
  29.8 3.6 reshape_squeeze.11
  33.5 3.2 copy.70
  36.7 3.3 copy.72
  40.0 3.1 reshape_squeeze.12
  43.0 3.2 copy.71
  46.2 3.3 copy.73
  49.5 3.1 reshape_squeeze.10
  52.6 3.2 copy.69
  55.8 3.4 copy.74
  59.2 6.8 %fusion.48 = (f32[2,88,64]{2,1,0:T(8,128)}, f32[2,88,64,64]{2,3,1,0:T(8,128)}) fusion(bf16[2,64,88,32]{1,3,2,0:T(8,128)(2,1)S(1)} %copy-done.7, bf16[2,64,88,32]{1,3,2,0:T(8,128)(2,1)} %copy.73), kind=kOutput, calls=%fused_computation.67 | convolution fusion | flops 48300096 | bytes 4370432 | tf_op jit(solution)/shard_map/sub | solution.py:22
  66.0 3.9 fusion.14
  69.9 5.5 copy.76
  75.4 3.8 reshape_reshape.6
  79.2 1.9 collective-permute-start.1
  81.2 4.3 collective-permute-done.1
  85.5 0.2 fusion.21
  85.7 1.4 fusion.22
  87.0 0.0 all-gather.3.cloned.1.call-update
  87.1 0.0 all-gather.5.cloned.1.call-start
  87.1 0.7 all-gather.5.cloned.1.call-update
  87.8 214.8 %all-gather.3.cloned.1.call-done = bf16[16,128,2816]{2,1,0:T(8,128)(2,1)} async-done(((bf16[1,128,2816]{2,1,0:T(8,128)(2,1)}), bf16[16,128,2816]{2,1,0:T(8,128)(2,1)}) %all-gather.3.cloned.1.call-update) | async-done | bytes 11534352 | tf_op jit(solution)/shard_map/all_gather | solution.py:96
  302.6 6.9 %convolution_convert_fusion = bf16[16,128,176]{1,2,0:T(8,128)(2,1)S(1)} fusion(bf16[16,128,2816]{2,1,0:T(8,128)(2,1)} %all-gather.3.cloned.1.call-done, bf16[2816,176]{0,1:T(8,128)(2,1)S(1)} %copy-done), kind=kOutput, calls=%fused_computation.27 | convolution fusion | flops 2030403584 | bytes 13246464 | tf_op jit(solution)/shard_map/kph,hc->kpc/dot_general | solution.py:94
  309.5 0.5 copy.79
  310.0 1.3 copy.80
  311.3 8.2 %all-to-all-start = ((bf16[16,8,16,176]{3,1,0,2:T(8,128)(2,1)}), bf16[16,8,16,176]{3,1,0,2:T(8,128)(2,1)S(1)}, u32[]{:S(2)}, u32[]{:S(2)}) async-start(bf16[16,8,16,176]{3,1,0,2:T(8,128)(2,1)} %copy.80), calls=%async_computation | async-start | bytes 2097152 | tf_op jit(solution)/shard_map/all_to_all | solution.py:101
  319.5 1.2 fusion.42
  320.7 0.3 reshape.164
  321.0 0.3 reshape.165
  321.4 0.3 reshape.166
  321.7 0.6 fusion.43
  322.3 1.5 convolution_multiply_fusion
  323.8 2.1 convolution_convert_fusion.2
  325.9 0.0 copy-start.9
  325.9 199.1 %all-gather.5.cloned.1.call-done = bf16[1024,1024]{1,0:T(8,128)(2,1)} async-done(((bf16[64,1024]{1,0:T(8,128)(2,1)}), bf16[1024,1024]{1,0:T(8,128)(2,1)}) %all-gather.5.cloned.1.call-update) | async-done | bytes 2097168 | tf_op jit(solution)/shard_map/all_gather | solution.py:92
  525.1 2.1 convolution_convert_fusion.1
  527.1 0.0 copy-start.11
  527.1 0.9 copy.86
  528.0 0.0 all-to-all-done
  528.0 10.0 %all-to-all-start.1 = ((bf16[1,8,16,1024]{3,1,0,2:T(8,128)(2,1)}), bf16[1,8,16,1024]{3,1,0,2:T(8,128)(2,1)S(1)}, u32[]{:S(2)}, u32[]{:S(2)}) async-start(bf16[1,8,16,1024]{3,1,0,2:T(8,128)(2,1)} %copy.86), calls=%async_computation.1 | async-start | bytes 524288 | tf_op jit(solution)/shard_map/all_to_all | solution.py:102
  538.0 0.2 add.81
  538.3 0.7 convert_element_type.102
  539.0 0.3 copy.87
  539.3 1.8 copy.81
  541.1 1.9 concatenate.31
  543.1 17.6 %all-to-all-done.1 = bf16[1,8,16,1024]{3,1,0,2:T(8,128)(2,1)S(1)} async-done(((bf16[1,8,16,1024]{3,1,0,2:T(8,128)(2,1)}), bf16[1,8,16,1024]{3,1,0,2:T(8,128)(2,1)S(1)}, u32[]{:S(2)}, u32[]{:S(2)}) %all-to-all-start.1) | async-done | bytes 262176 | tf_op jit(solution)/shard_map/all_to_all | solution.py:102
  560.7 0.1 maximum_convert_fusion
  560.8 3.0 reshape.169
  563.9 9.9 %fusion.51 = f32[8,60,16,16]{2,3,1,0:T(8,128)} fusion(f32[16,8,60,64]{3,2,1,0:T(8,128)} %reshape.169, f32[16,60,64]{2,0,1:T(8,128)S(1)} %copy.87), kind=kOutput, calls=%fused_computation.69 | convolution fusion | flops 16711680 | bytes 2703360 | tf_op jit(solution)/shard_map/tphd,sphd->phts/dot_general | solution.py:57
  573.8 3.3 copy.90
  577.1 13.3 %fusion.49 = (f32[8,60,16]{1,2,0:T(8,128)S(1)}, f32[8,60,16,16]{1,3,2,0:T(8,128)S(1)}) fusion(f32[8,60,16,16]{1,3,2,0:T(8,128)S(1)} %copy.90, pred[8,16,16]{2,1,0:T(8,128)(4,1)S(1)} %broadcast_or_fusion), kind=kOutput, calls=%fused_computation.68 | output fusion | flops 614415 | bytes 1015808 | tf_op jit(solution)/shard_map/sub | solution.py:65
  590.4 0.1 divide_convert_fusion.6
  590.6 1.9 copy.91
  592.5 8.5 %multiply_reduce_fusion.1 = (f32[16,8]{0,1:T(8,128)S(1)}, f32[16,8,60,64]{3,0,2,1:T(8,128)S(1)}) fusion(bf16[8,60,16,16]{3,2,1,0:T(8,128)(2,1)S(1)} %copy.91, f32[16,60,64]{2,0,1:T(8,128)S(1)} %copy.87, f32[16,8,60,64]{3,2,1,0:T(8,128)} %reshape.169), kind=kOutput, calls=%fused_computation.11 | convolution fusion | flops 19660672 | bytes 4424192 | tf_op jit(solution)/shard_map/phts,sphd->tphd/dot_general | solution.py:68
  601.0 3.2 copy.92
  604.1 3.6 reshape.168
  607.8 0.1 copy.93
  607.8 2.5 fusion.19
  (28 shorter events, 0.1 us)
Async XLA Ops:
  6.5 296.1 %copy-start = (bf16[2816,176]{0,1:T(8,128)(2,1)S(1)}, bf16[2816,176]{0,1:T(8,128)(2,1)}, u32[]{:S(2)}) copy-start(bf16[2816,176]{0,1:T(8,128)(2,1)} %param.10) | copy-start | bytes 2973700
  6.5 19.7 %copy-start.3 = (bf16[3,1,8,16,2816]{4,3,2,1,0:T(8,128)(2,1)S(1)}, bf16[3,1,8,16,2816]{4,3,2,1,0:T(8,128)(2,1)}, u32[]{:S(2)}) copy-start(bf16[3,1,8,16,2816]{4,3,2,1,0:T(8,128)(2,1)} %param.8) | copy-start | bytes 6488068
  6.5 296.1 %all-gather.3.cloned.1.call-start = ((), (), s32[]{:S(2)}) async-start(), calls=%async_computation.2 | async-start | bytes 12255232 | tf_op jit(solution)/shard_map/all_gather | solution.py:96
  9.0 17.2 %collective-permute-start = (bf16[3,1,4,16,2816]{4,3,2,1,0:T(8,128)(2,1)}, bf16[3,1,4,16,2816]{4,3,2,1,0:T(8,128)(2,1)}, u32[]{:S(2)}, u32[]{:S(2)}) collective-permute-start(bf16[3,1,4,16,2816]{4,3,2,1,0:T(8,128)(2,1)} %slice.30), channel_id=1, source_target_pairs={{0,496},{16,0},{32,16},{48,32},{64,48},{80,64},{96,80},{112,96},{1... | collective-permute-start | bytes 3244040 | tf_op jit(solution)/shard_map/ppermute | solution.py:16
  55.8 3.4 copy-start.7
  79.2 6.3 %collective-permute-start.1 = (bf16[4,16,2816]{2,1,0:T(8,128)(2,1)S(1)}, bf16[4,16,2816]{2,1,0:T(8,128)(2,1)S(1)}, u32[]{:S(2)}, u32[]{:S(2)}) collective-permute-start(bf16[4,16,2816]{2,1,0:T(8,128)(2,1)S(1)} %copy_bitcast_fusion.1), channel_id=1, source_target_pairs={{0,16},{16,32},{32,48},{48,64},{64,80},{80,96},{96,112},{112,128},... | collective-permute-start | bytes 1081352 | tf_op jit(solution)/shard_map/ppermute | solution.py:16
  87.1 438.0 %all-gather.5.cloned.1.call-start = ((), (), s32[]{:S(2)}) async-start(), calls=%async_computation.3 | async-start | bytes 2228224 | tf_op jit(solution)/shard_map/all_gather | solution.py:92
  311.3 216.7 %all-to-all-start = ((bf16[16,8,16,176]{3,1,0,2:T(8,128)(2,1)}), bf16[16,8,16,176]{3,1,0,2:T(8,128)(2,1)S(1)}, u32[]{:S(2)}, u32[]{:S(2)}) async-start(bf16[16,8,16,176]{3,1,0,2:T(8,128)(2,1)} %copy.80), calls=%async_computation | async-start | bytes 2097152 | tf_op jit(solution)/shard_map/all_to_all | solution.py:101
  325.9 212.1 %copy-start.9 = (bf16[16,3840]{1,0:T(8,128)(2,1)S(1)}, bf16[16,3840]{1,0:T(8,128)(2,1)}, u32[]{:S(2)}) copy-start(bf16[16,3840]{1,0:T(8,128)(2,1)} %param.14) | copy-start | bytes 368644
  527.1 12.2 %copy-start.11 = (s32[16,8,1]{0,2,1:T(1,128)S(1)}, s32[16,8,1]{0,2,1:T(1,128)}, u32[]{:S(2)}) copy-start(s32[16,8,1]{0,2,1:T(1,128)} %param.13) | copy-start | bytes 1540
  528.0 11.3 %copy-start.4 = (bf16[16,8,16,176]{3,1,0,2:T(8,128)(2,1)}, bf16[16,8,16,176]{3,1,0,2:T(8,128)(2,1)S(1)}, u32[]{:S(2)}) copy-start(bf16[16,8,16,176]{3,1,0,2:T(8,128)(2,1)S(1)} %all-to-all-done) | copy-start | bytes 2162692
  528.0 32.7 %all-to-all-start.1 = ((bf16[1,8,16,1024]{3,1,0,2:T(8,128)(2,1)}), bf16[1,8,16,1024]{3,1,0,2:T(8,128)(2,1)S(1)}, u32[]{:S(2)}, u32[]{:S(2)}) async-start(bf16[1,8,16,1024]{3,1,0,2:T(8,128)(2,1)} %copy.86), calls=%async_computation.1 | async-start | bytes 524288 | tf_op jit(solution)/shard_map/all_to_all | solution.py:102
  543.1 20.8 %copy-start.2 = (bf16[16,8,1,2816]{3,1,0,2:T(8,128)(2,1)}, bf16[16,8,1,2816]{3,1,0,2:T(8,128)(2,1)S(1)}, u32[]{:S(2)}) copy-start(bf16[16,8,1,2816]{3,1,0,2:T(8,128)(2,1)S(1)} %concatenate.31) | copy-start | bytes 2162692
  560.7 3.2 copy-start.5
  604.1 3.7 copy-start.6
  604.1 3.7 copy-start.8
  604.1 3.7 copy-start.10
  604.1 6.2 copy-start.1
Sparse Core Ops, SparseCore 0:
  87.2 215.3 all-gather.2
  305.6 219.3 all-gather.4
where the time goes:
time: 621 us; the launch traced here: 617 us
  waiting for transfers between devices  451 us (73%)
  local copies, waits for them, and re-layouts  65.4 us (11%)
  matrix products  42.3 us (7%)
  starting transfers between devices  22.7 us (4%)
  other arithmetic  21.8 us (4%)
  between operations  14.7 us (2%)
    all_gather x1, waiting for transfers between devices, per_device(): lax.all_gather(hr_flat[None], 'date', axis=0, tiled=True)  215 us
    all_gather x1, waiting for transfers between devices, per_device(): lax.all_gather(s_proj, 'date', axis=0, tiled=True)  199 us
    ppermute x2, waiting for transfers between devices, passed_along(): return lax.ppermute(x, axis, [(i, (i + by) % size) for i in range(size)])  18.3 us
    all_to_all x1, waiting for transfers between devices, per_device(): lax.all_to_all(s_out, 'date', split_axis=2, concat_axis=0, tiled=True)  17.6 us
    sub x1, other arithmetic, temporal(): scores = scores - jnp.max(scores, axis=-1, keepdims=True)  13.3 us
  transfers between devices with their start and end apart: 6, of which 5 were waited for; matrix products, arithmetic and copies ran while one was open for 4% of the time, Pallas kernels for 0%

commit v1 on v0

v1 whole, which is shorter than its diff:
```python
import functools

import jax
import jax.numpy as jnp
from jax import lax
from jax.experimental import pallas as pl
from jax.experimental.pallas import tpu as pltpu
from jax.sharding import Mesh
from jax.sharding import PartitionSpec as P

HRW = 2816
SW = 1024
HR_HEAD = 32
S_HEAD = 64
T_HEAD = 64
WIN = 8
COLS = 16
ROWS = 8
DATES = 16
F = HRW + SW
TOK = ROWS * COLS
LANES = 128
MARGIN = WIN // 2
LOG2E = 1.4426950408889634
OFF = -1e30

SPACE = ("y", "zl", "core")
DATE = ("x", "zh")


def iota2(shape, dim):
    return lax.broadcasted_iota(jnp.int32, shape, dim)


def attend_group(q, k, v, head_dim, bias, scale):
    heads = LANES // head_dim
    head_of = iota2((TOK, LANES), 1) // head_dim
    mine = [head_of == h for h in range(heads)]
    zero = jnp.zeros_like(k)
    k_heads = jnp.concatenate([jnp.where(m, k, zero) for m in mine], axis=0)
    scores = lax.dot_general(
        q, k_heads, (((1,), (1,)), ((), ())), preferred_element_type=jnp.float32
    )
    weights = []
    for h in range(heads):
        one = scores[:, h * TOK : (h + 1) * TOK] * (scale * LOG2E)
        if bias is not None:
            one = one + bias
        top = jnp.max(one, axis=1, keepdims=True)
        weights.append(jnp.exp2(one - top).astype(jnp.bfloat16))
    weights = jnp.concatenate(weights, axis=1)
    v_heads = jnp.concatenate([jnp.where(m, v, zero) for m in mine], axis=0)
    ones = jnp.concatenate([m.astype(jnp.float32) for m in mine], axis=0).astype(jnp.bfloat16)
    both = jnp.dot(
        weights,
        jnp.concatenate([v_heads, ones], axis=1),
        preferred_element_type=jnp.float32,
    )
    return both[:, :LANES] / both[:, LANES:]


def window_kernel(offset_ref, own_ref, below_ref, out_ref, next_ref, stack):
    offset = offset_ref[0]
    stack[:, :TOK] = own_ref[...]
    stack[:, TOK:] = below_ref[...]
    start = pl.multiple_of(offset * COLS, COLS)
    q, k, v = [stack[i, pl.ds(start, TOK), :] for i in range(3)]
    span = COLS
    col_q = iota2((TOK, TOK), 0) % span
    col_k = iota2((TOK, TOK), 1) % span
    win_q = ((col_q - offset + span) % span) // WIN
    win_k = ((col_k - offset + span) % span) // WIN
    bias = jnp.where(win_q == win_k, 0.0, OFF)
    mixed = attend_group(q, k, v, HR_HEAD, bias, 1.0 / HR_HEAD**0.5).astype(jnp.bfloat16)
    src_row = iota2((TOK, TOK), 1) // COLS + offset
    src_col = iota2((TOK, TOK), 1) % COLS
    dst = iota2((TOK, TOK), 0)
    place = jnp.where((dst // ROWS == src_col) & (dst % ROWS == src_row), 1.0, 0.0)
    out_ref[...] = jnp.dot(
        place.astype(jnp.bfloat16), mixed, preferred_element_type=jnp.float32
    ).astype(jnp.bfloat16)
    half = TOK // 2
    src_row = iota2((half, TOK), 1) // COLS + offset
    src_col = iota2((half, TOK), 1) % COLS
    dst = iota2((half, TOK), 0)
    place = jnp.where(
        (dst // MARGIN == src_col) & (dst % MARGIN + ROWS == src_row), 1.0, 0.0
    )
    next_ref[...] = jnp.dot(
        place.astype(jnp.bfloat16), mixed, preferred_element_type=jnp.float32
    ).astype(jnp.bfloat16)


def window_attention(offset, own, below):
    half = TOK // 2
    groups = HRW // LANES
    return pl.pallas_call(
        window_kernel,
        grid=(groups,),
        in_specs=[
            pl.BlockSpec(memory_space=pltpu.SMEM),
            pl.BlockSpec((3, TOK, LANES), lambda i: (0, 0, i)),
            pl.BlockSpec((3, half, LANES), lambda i: (0, 0, i)),
        ],
        out_specs=[
            pl.BlockSpec((TOK, LANES), lambda i: (0, i)),
            pl.BlockSpec((half, LANES), lambda i: (0, i)),
        ],
        out_shape=[
            jax.ShapeDtypeStruct((TOK, HRW), jnp.bfloat16),
            jax.ShapeDtypeStruct((half, HRW), jnp.bfloat16),
        ],
        scratch_shapes=[pltpu.VMEM((3, TOK + half, LANES), jnp.bfloat16)],
        name="window_attention",
    )(offset, own, below)


def tile_kernel(own_ref, out_ref):
    mixed = attend_group(
        own_ref[0], own_ref[1], own_ref[2], S_HEAD, None, 1.0 / S_HEAD**0.5
    ).astype(jnp.bfloat16)
    src = iota2((TOK, TOK), 1)
    dst = iota2((TOK, TOK), 0)
    place = jnp.where((dst // ROWS == src % COLS) & (dst % ROWS == src // COLS), 1.0, 0.0)
    out_ref[...] = jnp.dot(
        place.astype(jnp.bfloat16), mixed, preferred_element_type=jnp.float32
    ).astype(jnp.bfloat16)


def tile_attention(own):
    return pl.pallas_call(
        tile_kernel,
        grid=(SW // LANES,),
        in_specs=[pl.BlockSpec((3, TOK, LANES), lambda i: (0, 0, i))],
        out_specs=pl.BlockSpec((TOK, LANES), lambda i: (0, i)),
        out_shape=jax.ShapeDtypeStruct((TOK, SW), jnp.bfloat16),
        name="tile_attention",
    )(own)


BLOCK = 256
HR_BLOCKS = HRW // BLOCK
S_BLOCKS = SW // BLOCK


def merge_kernel(
    hr_ref, s_ref, hr_w_ref, s_w_ref, valid_ref, embed_ref, gain_ref, out_ref, mixed_ref, out_tmp
):
    step = pl.program_id(0)

    def one_block(projected):
        col = pl.ds(pl.multiple_of(step * BLOCK, BLOCK), BLOCK)
        embed = embed_ref[...].astype(jnp.float32)
        embed = jnp.broadcast_to(embed[:, None, :], (DATES, ROWS, BLOCK)).reshape(TOK, BLOCK)
        joined = (projected.astype(jnp.bfloat16).astype(jnp.float32) + embed).astype(jnp.bfloat16)
        query = iota2((TOK, TOK), 0)
        key = iota2((TOK, TOK), 1)
        keep = (query % ROWS == key % ROWS) & ((valid_ref[...] > 0) | (query == key))
        bias = jnp.where(keep, 0.0, OFF)
        for g in range(BLOCK // LANES):
            part = joined[:, g * LANES : (g + 1) * LANES]
            mixed = part.astype(jnp.float32) + attend_group(
                part, part, part, T_HEAD, bias, 1.0 / T_HEAD
            )
            mixed_ref[step * (BLOCK // LANES) + g] = mixed

    @pl.when(step < HR_BLOCKS)
    def _():
        one_block(
            lax.dot_general(
                hr_ref[...],
                hr_w_ref[...],
                (((1,), (1,)), ((), ())),
                preferred_element_type=jnp.float32,
            )
        )

    @pl.when(step >= HR_BLOCKS)
    def _():
        one_block(jnp.dot(s_ref[...], s_w_ref[...], preferred_element_type=jnp.float32))

    @pl.when(step == HR_BLOCKS + S_BLOCKS - 1)
    def _():
        total = jnp.zeros((TOK, LANES), jnp.float32)
        for g in range(F // LANES):
            total += mixed_ref[g] * mixed_ref[g]
        scale = lax.rsqrt(jnp.sum(total, axis=1, keepdims=True) * (1.0 / F) + 1e-06)
        for g in range(F // LANES):
            lanes = slice(g * LANES, (g + 1) * LANES)
            out_ref[:, lanes] = (mixed_ref[g] * scale * gain_ref[:, lanes]).astype(jnp.bfloat16)


def merge(hr_tokens, s_tokens, hr_weights, s_weights, valid, embed, gain):
    return pl.pallas_call(
        merge_kernel,
        grid=(HR_BLOCKS + S_BLOCKS,),
        in_specs=[
            pl.BlockSpec((TOK, HRW), lambda i: (0, 0)),
            pl.BlockSpec((TOK, SW), lambda i: (0, 0)),
            pl.BlockSpec((BLOCK, HRW), lambda i: (jnp.minimum(i, HR_BLOCKS - 1), 0)),
            pl.BlockSpec((SW, BLOCK), lambda i: (0, jnp.maximum(i - HR_BLOCKS, 0))),
            pl.BlockSpec((1, TOK), lambda i: (0, 0)),
            pl.BlockSpec((DATES, BLOCK), lambda i: (0, i)),
            pl.BlockSpec((1, F), lambda i: (0, 0)),
        ],
        out_specs=pl.BlockSpec((TOK, F), lambda i: (0, 0)),
        out_shape=jax.ShapeDtypeStruct((TOK, F), jnp.bfloat16),
        scratch_shapes=[
            pltpu.VMEM((F // LANES, TOK, LANES), jnp.float32),
            pltpu.VMEM((8, LANES), jnp.float32),
        ],
        compiler_params=pltpu.CompilerParams(vmem_limit_bytes=40 * 2**20),
        name="merge",
    )(hr_tokens, s_tokens, hr_weights, s_weights, valid, embed, gain)


def per_device(hr_qkv, s_qkv, hr_proj, s_proj, shifts, cloud_valid, date_embed, norm_gain):
    space = lax.axis_size(SPACE)
    half = TOK // 2
    own = hr_qkv.reshape(3, TOK, HRW)
    below = lax.ppermute(
        own[:, :half], SPACE, [(i, (i - 1) % space) for i in range(space)]
    )
    hr_weights = lax.all_gather(hr_proj.T, DATE, axis=0, tiled=True)
    s_weights = lax.all_gather(s_proj, DATE, axis=0, tiled=True)

    tile_out = tile_attention(s_qkv.reshape(3, TOK, SW))
    s_tokens = lax.all_to_all(
        tile_out.reshape(COLS, ROWS, SW), DATE, split_axis=0, concat_axis=0, tiled=True
    )

    window_out, passed = window_attention(shifts, own, below)
    above = lax.ppermute(passed, SPACE, [(i, (i + 1) % space) for i in range(space)])
    window_out = window_out.reshape(COLS, ROWS, HRW)
    top = window_out[:, :MARGIN] + above.reshape(COLS, MARGIN, HRW)
    window_out = jnp.concatenate([top, window_out[:, MARGIN:]], axis=1)
    hr_tokens = lax.all_to_all(window_out, DATE, split_axis=0, concat_axis=0, tiled=True)

    out = merge(
        hr_tokens.reshape(TOK, HRW),
        s_tokens.reshape(TOK, SW),
        hr_weights,
        s_weights,
        cloud_valid.reshape(1, TOK),
        date_embed,
        norm_gain.reshape(1, F),
    )
    return out.reshape(DATES, ROWS, 1, F)


def solution(mesh):
    fine = Mesh(mesh.devices.reshape(4, 4, 2, 4, 4), SPACE + DATE)
    in_specs = (
        P(None, DATE, SPACE, None, None),
        P(None, DATE, SPACE, None, None),
        P(None, DATE),
        P(DATE, None),
        P(DATE),
        P(None, SPACE, DATE),
        P(),
        P(),
    )
    out_specs = P(None, SPACE, DATE, None)
    return jax.shard_map(
        per_device, mesh=fine, in_specs=in_specs, out_specs=out_specs, check_vma=False
    )
```

time: 621 us -> 545 us (0.88)
  the two profiles are of different devices: /device:TPU:41 before, /device:TPU:15 now
where the time goes in v1:
time: 545 us; the launch traced here: 543 us
  waiting for transfers between devices  450 us (83%)
  Pallas kernels  46.1 us (8%)
  starting transfers between devices  27 us (5%)
  between operations  14.1 us (3%)
    all_gather x1, waiting for transfers between devices, per_device(): hr_weights = lax.all_gather(hr_proj.T, DATE, axis=0, tiled=True)  360 us
    all_to_all x1, waiting for transfers between devices, per_device(): lax.all_to_all(tile_out.reshape(COLS, ROWS, SW), DATE, split_axis=0, conc...  43.3 us
    all_to_all x1, waiting for transfers between devices, per_device(): lax.all_to_all(window_out, DATE, split_axis=0, concat_axis=0, tiled=True)  31.4 us
    pallas_call x1, Pallas kernels, merge(): pl.pallas_call(merge_kernel, grid=(HR_BLOCKS + S_BLOCKS,), in_specs=[pl.B...  21.3 us
    pallas_call x1, Pallas kernels, window_attention(): pl.pallas_call(window_kernel, grid=(groups,), in_specs=[pl.BlockSpec(memo...  17.9 us
    all_to_all x1, starting transfers between devices, per_device(): lax.all_to_all(tile_out.reshape(COLS, ROWS, SW), DATE, split_axis=0, conc...  17 us
    ppermute x1, waiting for transfers between devices, per_device(): lax.ppermute(own[:, :half], SPACE, [(i, (i - 1) % space) for i in range(s...  13.7 us
  transfers between devices with their start and end apart: 6, of which 5 were waited for; matrix products, arithmetic and copies ran while one was open for 1% of the time, Pallas kernels for 5%

profile of v1, /device:TPU:15, one launch (start us, length us, event | category | flops | bytes accessed | tf_op | source)
XLA Modules:
  0.0 543.0 jit_solution(10904060607635693101)
XLA Ops:
  6.5 0.0 all-gather.5.cloned.1.call-start
  6.5 0.7 all-gather.5.cloned.1.call-update
  7.3 0.0 all-gather.3.cloned.1.call-start
  7.3 0.7 all-gather.3.cloned.1.call-update
  8.0 1.3 slice.12
  9.3 2.6 collective-permute-start
  12.6 13.7 %collective-permute-done.below_ref = bf16[3,64,2816]{2,1,0:T(8,128)(2,1)S(1)} collective-permute-done((bf16[3,64,2816]{2,1,0:T(8,128)(2,1)S(1)}, bf16[3,64,2816]{2,1,0:T(8,128)(2,1)S(1)}, u32[]{:S(2)}, u32[]{:S(2)}) %collective-permute-start) | collective-permute-done | bytes 1081376 | tf_op jit(solution)/shard_map/ppermute | solution.py:221
  26.3 0.0 copy-start.2
  26.3 1.0 copy-done.2
  27.2 17.9 %window_attention.1 = (bf16[128,2816]{1,0:T(8,128)(2,1)}, bf16[64,2816]{1,0:T(8,128)(2,1)}) custom-call(s32[1]{0:T(128)S(6)} %copy.13.offset_ref, bf16[3,128,2816]{2,1,0:T(8,128)(2,1)} %bitcast.15, bf16[3,64,2816]{2,1,0:T(8,128)(2,1)} %copy-done.2), custom_call_target="tpu_custom_call" | custom-call | tf_op jit(solution)/shard_map/window_attention/pallas_call | solution.py:97
  45.1 0.0 copy-start.3
  45.1 2.0 collective-permute-start.1
  47.1 7.0 %tile_attention.1 = bf16[128,1024]{1,0:T(8,128)(2,1)} custom-call(bf16[3,128,1024]{2,1,0:T(8,128)(2,1)} %bitcast.18), custom_call_target="tpu_custom_call" | custom-call | tf_op jit(solution)/shard_map/tile_attention/pallas_call | solution.py:131
  54.1 17.0 %all-to-all-start.1 = ((bf16[16,8,1024]{2,1,0:T(8,128)(2,1)}), bf16[16,8,1024]{2,1,0:T(8,128)(2,1)S(1)}, u32[]{:S(2)}, u32[]{:S(2)}) async-start(bf16[16,8,1024]{2,1,0:T(8,128)(2,1)} %bitcast.16), calls=%async_computation.1 | async-start | bytes 524288 | tf_op jit(solution)/shard_map/all_to_all | solution.py:228
  71.1 0.0 collective-permute-done.1
  71.1 0.1 reshape.32
  71.2 0.0 copy-done.3
  71.2 0.4 slice_add_fusion
  71.6 0.0 copy-start.4
  71.6 0.0 copy-start.5
  71.6 0.0 copy-start.1
  71.6 1.2 pad_maximum_fusion
  72.8 43.3 %all-to-all-done.1 = bf16[16,8,1024]{2,1,0:T(8,128)(2,1)S(1)} async-done(((bf16[16,8,1024]{2,1,0:T(8,128)(2,1)}), bf16[16,8,1024]{2,1,0:T(8,128)(2,1)S(1)}, u32[]{:S(2)}, u32[]{:S(2)}) %all-to-all-start.1) | async-done | bytes 262176 | tf_op jit(solution)/shard_map/all_to_all | solution.py:228
  116.1 5.3 all-to-all-start
  121.4 0.0 copy-done.4
  121.5 0.0 copy-done.5
  121.5 0.1 copy.11
  121.5 0.1 reshape.37.valid_ref
  121.6 0.2 all-gather.5.cloned.1.call-done.s_w_ref
  121.9 31.4 %all-to-all-done = bf16[16,8,2816]{2,1,0:T(8,128)(2,1)S(1)} async-done(((bf16[16,8,2816]{2,1,0:T(8,128)(2,1)}), bf16[16,8,2816]{2,1,0:T(8,128)(2,1)S(1)}, u32[]{:S(2)}, u32[]{:S(2)}) %all-to-all-start) | async-done | bytes 720928 | tf_op jit(solution)/shard_map/all_to_all | solution.py:237
  153.3 360.0 %all-gather.3.cloned.1.call-done.hr_w_ref = bf16[2816,2816]{1,0:T(8,128)(2,1)} async-done(((bf16[176,2816]{1,0:T(8,128)(2,1)}), bf16[2816,2816]{1,0:T(8,128)(2,1)}) %all-gather.3.cloned.1.call-update) | async-done | bytes 15859728 | tf_op jit(solution)/shard_map/all_gather | solution.py:224
  513.3 0.0 copy-done.1
  513.3 0.0 copy-start
  513.3 1.6 copy-done
  514.8 21.3 %merge.1 = bf16[128,3840]{1,0:T(8,128)(2,1)} custom-call(bf16[128,2816]{1,0:T(8,128)(2,1)S(1)} %bitcast.12, bf16[128,1024]{1,0:T(8,128)(2,1)S(1)} %bitcast.13, bf16[2816,2816]{1,0:T(8,128)(2,1)} %all-gather.3.cloned.1.call-done.hr_w_ref, bf16[1024,1024]{1,0:T(8,128)(2,1)S(1)} %copy-done, s32[1,128]{1,0:T(1,128)S(1)} %reshape.37.valid_ref, ...), custom_call_target="tpu_custom_call" | custom-call | tf_op jit(solution)/shard_map/merge/pallas_call | solution.py:194
  (1 shorter events, 0.0 us)
Async XLA Ops:
  6.5 115.3 %all-gather.5.cloned.1.call-start = ((), (), s32[]{:S(2)}) async-start(), calls=%async_computation.3 | async-start | bytes 2228224 | tf_op jit(solution)/shard_map/all_gather | solution.py:225
  7.3 506.0 %all-gather.3.cloned.1.call-start = ((), (), s32[]{:S(2)}) async-start(), calls=%async_computation.2 | async-start | bytes 16850944 | tf_op jit(solution)/shard_map/all_gather | solution.py:224
  9.3 16.9 %collective-permute-start = (bf16[3,64,2816]{2,1,0:T(8,128)(2,1)S(1)}, bf16[3,64,2816]{2,1,0:T(8,128)(2,1)S(1)}, u32[]{:S(2)}, u32[]{:S(2)}) collective-permute-start(bf16[3,64,2816]{2,1,0:T(8,128)(2,1)S(1)} %slice.12), channel_id=1, source_target_pairs={{0,496},{16,0},{32,16},{48,32},{64,48},{80,64},{96,80},{112,96},{1... | collective-permute-start | bytes 3244040 | tf_op jit(solution)/shard_map/ppermute | solution.py:221
  26.3 1.0 copy-start.2
  45.1 26.1 %copy-start.3 = (bf16[128,2816]{1,0:T(8,128)(2,1)S(1)}, bf16[128,2816]{1,0:T(8,128)(2,1)}, u32[]{:S(2)}) copy-start(bf16[128,2816]{1,0:T(8,128)(2,1)} %get-tuple-element.7) | copy-start | bytes 2162692
  45.1 26.0 %collective-permute-start.1 = (bf16[64,2816]{1,0:T(8,128)(2,1)}, bf16[64,2816]{1,0:T(8,128)(2,1)S(1)}, u32[]{:S(2)}, u32[]{:S(2)}) collective-permute-start(bf16[64,2816]{1,0:T(8,128)(2,1)} %get-tuple-element.8), channel_id=1, source_target_pairs={{0,16},{16,32},{32,48},{48,64},{64,80},{80,96},{96,112},{112,128},... | collective-permute-start | bytes 1081352 | tf_op jit(solution)/shard_map/ppermute | solution.py:233
  54.1 62.0 %all-to-all-start.1 = ((bf16[16,8,1024]{2,1,0:T(8,128)(2,1)}), bf16[16,8,1024]{2,1,0:T(8,128)(2,1)S(1)}, u32[]{:S(2)}, u32[]{:S(2)}) async-start(bf16[16,8,1024]{2,1,0:T(8,128)(2,1)} %bitcast.16), calls=%async_computation.1 | async-start | bytes 524288 | tf_op jit(solution)/shard_map/all_to_all | solution.py:228
  71.6 49.8 %copy-start.4 = (f32[3840]{0:T(1024)S(1)}, f32[3840]{0:T(1024)}, u32[]{:S(2)}) copy-start(f32[3840]{0:T(1024)} %param.15) | copy-start | bytes 46084
  71.6 49.9 %copy-start.5 = (s32[16,8,1]{0,2,1:T(1,128)S(1)}, s32[16,8,1]{0,2,1:T(1,128)}, u32[]{:S(2)}) copy-start(s32[16,8,1]{0,2,1:T(1,128)} %param.13) | copy-start | bytes 1540
  71.6 441.6 %copy-start.1 = (bf16[16,3840]{1,0:T(8,128)(2,1)S(1)}, bf16[16,3840]{1,0:T(8,128)(2,1)}, u32[]{:S(2)}) copy-start(bf16[16,3840]{1,0:T(8,128)(2,1)} %embed_ref.1) | copy-start | bytes 368644
  116.1 37.1 %all-to-all-start = ((bf16[16,8,2816]{2,1,0:T(8,128)(2,1)}), bf16[16,8,2816]{2,1,0:T(8,128)(2,1)S(1)}, u32[]{:S(2)}, u32[]{:S(2)}) async-start(bf16[16,8,2816]{2,1,0:T(8,128)(2,1)} %pad_maximum_fusion), calls=%async_computation | async-start | bytes 1441792 | tf_op jit(solution)/shard_map/all_to_all | solution.py:237
  513.3 1.6 copy-start
Sparse Core Ops, SparseCore 0:
  10.4 111.4 all-gather.4
  124.9 388.2 all-gather.2

commit v2 on v1

v2 whole, which is shorter than its diff:
```python
import functools

import jax
import jax.numpy as jnp
from jax import lax
from jax.experimental import pallas as pl
from jax.experimental.pallas import tpu as pltpu
from jax.sharding import Mesh
from jax.sharding import PartitionSpec as P

HRW = 2816
SW = 1024
HR_HEAD = 32
S_HEAD = 64
T_HEAD = 64
WIN = 8
COLS = 16
ROWS = 8
DATES = 16
F = HRW + SW
TOK = ROWS * COLS
LANES = 128
MARGIN = WIN // 2
LOG2E = 1.4426950408889634
OFF = -1e30

SPACE = ("y", "zl", "core")
DATE = ("x", "zh")


def iota2(shape, dim):
    return lax.broadcasted_iota(jnp.int32, shape, dim)


def head_masks(head_dim):
    head_of = iota2((TOK, LANES), 1) // head_dim
    return [head_of == h for h in range(LANES // head_dim)]


def attend_group(q, k, v, masks, ones, bias, scale):
    zero = jnp.zeros_like(k)
    k_heads = jnp.concatenate([jnp.where(m, k, zero) for m in masks], axis=0)
    scores = lax.dot_general(
        q, k_heads, (((1,), (1,)), ((), ())), preferred_element_type=jnp.float32
    )
    weights = []
    for h in range(len(masks)):
        one = scores[:, h * TOK : (h + 1) * TOK] * (scale * LOG2E)
        if bias is not None:
            one = one + bias
        top = jnp.max(one, axis=1, keepdims=True)
        weights.append(jnp.exp2(one - top).astype(jnp.bfloat16))
    weights = jnp.concatenate(weights, axis=1)
    v_heads = jnp.concatenate([jnp.where(m, v, zero) for m in masks], axis=0)
    both = jnp.dot(
        weights,
        jnp.concatenate([v_heads, ones], axis=1),
        preferred_element_type=jnp.float32,
    )
    return both[:, :LANES] / both[:, LANES:]


def ones_of(masks):
    return jnp.concatenate([m.astype(jnp.float32) for m in masks], axis=0).astype(jnp.bfloat16)


def place_rows(place, mixed):
    return jnp.dot(
        jnp.where(place, 1.0, 0.0).astype(jnp.bfloat16),
        mixed,
        preferred_element_type=jnp.float32,
    ).astype(jnp.bfloat16)


WIN_BLOCKS = 2
WIN_LANES = HRW // WIN_BLOCKS


def window_kernel(offset_ref, own_ref, below_ref, out_ref, next_ref, stack, mixed):
    offset = offset_ref[0]
    stack[:, :TOK] = own_ref[...]
    stack[:, TOK:] = below_ref[...]
    start = pl.multiple_of(offset * COLS, COLS)
    col_q = iota2((TOK, TOK), 0) % COLS
    col_k = iota2((TOK, TOK), 1) % COLS
    win_q = ((col_q - offset + COLS) % COLS) // WIN
    win_k = ((col_k - offset + COLS) % COLS) // WIN
    bias = jnp.where(win_q == win_k, 0.0, OFF)
    masks = head_masks(HR_HEAD)
    ones = ones_of(masks)
    for g in range(WIN_LANES // LANES):
        lanes = slice(g * LANES, (g + 1) * LANES)
        q, k, v = [stack[i, pl.ds(start, TOK), lanes] for i in range(3)]
        mixed[:, lanes] = attend_group(
            q, k, v, masks, ones, bias, 1.0 / HR_HEAD**0.5
        ).astype(jnp.bfloat16)
    src_row = iota2((TOK, TOK), 1) // COLS + offset
    src_col = iota2((TOK, TOK), 1) % COLS
    dst = iota2((TOK, TOK), 0)
    out_ref[...] = place_rows(
        (dst // ROWS == src_col) & (dst % ROWS == src_row), mixed[...]
    )
    half = TOK // 2
    src_row = iota2((half, TOK), 1) // COLS + offset
    src_col = iota2((half, TOK), 1) % COLS
    dst = iota2((half, TOK), 0)
    next_ref[...] = place_rows(
        (dst // MARGIN == src_col) & (dst % MARGIN + ROWS == src_row), mixed[...]
    )


def window_attention(offset, own, below):
    half = TOK // 2
    return pl.pallas_call(
        window_kernel,
        grid=(WIN_BLOCKS,),
        in_specs=[
            pl.BlockSpec(memory_space=pltpu.SMEM),
            pl.BlockSpec((3, TOK, WIN_LANES), lambda i: (0, 0, i)),
            pl.BlockSpec((3, half, WIN_LANES), lambda i: (0, 0, i)),
        ],
        out_specs=[
            pl.BlockSpec((TOK, WIN_LANES), lambda i: (0, i)),
            pl.BlockSpec((half, WIN_LANES), lambda i: (0, i)),
        ],
        out_shape=[
            jax.ShapeDtypeStruct((TOK, HRW), jnp.bfloat16),
            jax.ShapeDtypeStruct((half, HRW), jnp.bfloat16),
        ],
        scratch_shapes=[
            pltpu.VMEM((3, TOK + half, WIN_LANES), jnp.bfloat16),
            pltpu.VMEM((TOK, WIN_LANES), jnp.bfloat16),
        ],
        compiler_params=pltpu.CompilerParams(vmem_limit_bytes=24 * 2**20),
        name="window_attention",
    )(offset, own, below)


def tile_kernel(own_ref, out_ref, mixed):
    masks = head_masks(S_HEAD)
    ones = ones_of(masks)
    for g in range(SW // LANES):
        lanes = slice(g * LANES, (g + 1) * LANES)
        q, k, v = [own_ref[i, :, lanes] for i in range(3)]
        mixed[:, lanes] = attend_group(
            q, k, v, masks, ones, None, 1.0 / S_HEAD**0.5
        ).astype(jnp.bfloat16)
    src = iota2((TOK, TOK), 1)
    dst = iota2((TOK, TOK), 0)
    out_ref[...] = place_rows(
        (dst // ROWS == src % COLS) & (dst % ROWS == src // COLS), mixed[...]
    )


def tile_attention(own):
    return pl.pallas_call(
        tile_kernel,
        out_shape=jax.ShapeDtypeStruct((TOK, SW), jnp.bfloat16),
        scratch_shapes=[pltpu.VMEM((TOK, SW), jnp.bfloat16)],
        compiler_params=pltpu.CompilerParams(vmem_limit_bytes=16 * 2**20),
        name="tile_attention",
    )(own)


XS = 4
ZS = 4
SHARD = HRW // DATES
CHUNK = ZS * SHARD
CHUNK_PAD = 768
PIECE = 384
S_SHARD = SW // DATES
S_ROWS = S_SHARD // 2
PIECE_ROWS = SHARD + S_ROWS
NEAR_Y = (0, -1, 1, 2)
NEAR_Z = (-1, 1, 2)
PIECES = 8
LAST = HRW - PIECE
N_BLOCK = 256


def project_kernel(
    place_ref, own_ref, left_ref, right_ref, far_a_ref, far_b_ref, shard_ref, mine_ref, other_ref,
    out_ref, weights, sems,
):
    core, y, zh = place_ref[0], place_ref[1], place_ref[2]
    copies = []

    def fetch(src, piece, part):
        rows = pl.ds(pl.multiple_of(part * SHARD, SHARD), SHARD)
        copies.append(
            pltpu.make_async_copy(src, weights.at[piece, rows, :], sems.at[len(copies)])
        )
        copies[-1].start()

    for j in range(PIECES):
        fetch(shard_ref.at[:, pl.ds(min(j * PIECE, LAST), PIECE)], j, zh)
    for src, c in ((mine_ref, core), (other_ref, 1 - core)):
        for b, dy in enumerate(NEAR_Y):
            for s, dz in enumerate(NEAR_Z):
                fetch(
                    src.at[pl.ds((b * 3 + s) * PIECE_ROWS, SHARD), :],
                    c * 4 + lax.rem(y + dy + 4, 4),
                    lax.rem(zh + dz + 4, 4),
                )
    weights[:, CHUNK:, :] = jnp.zeros((PIECES, CHUNK_PAD - CHUNK, PIECE), jnp.bfloat16)
    tokens = jnp.concatenate(
        [own_ref[...], left_ref[...], right_ref[...], far_a_ref[...], far_b_ref[...]], axis=0
    )
    for copy in copies:
        copy.wait()
    for n in range(CHUNK_PAD // N_BLOCK):
        rows = slice(n * N_BLOCK, (n + 1) * N_BLOCK)
        part = [weights[j, rows, :] for j in range(PIECES - 1)]
        part.append(weights[PIECES - 1, rows, 2 * LANES :])
        result = lax.dot_general(
            tokens,
            jnp.concatenate(part, axis=1),
            (((1,), (1,)), ((), ())),
            preferred_element_type=jnp.float32,
        )
        result = result.reshape(XS, COLS, ROWS, N_BLOCK)
        result = jnp.concatenate([result[b] for b in range(XS)], axis=1)
        out_ref[:, :, rows] = result.astype(jnp.bfloat16)


def project(place, tokens, shard, mine, other):
    vmem = pl.BlockSpec(memory_space=pltpu.VMEM)
    hbm = pl.BlockSpec(memory_space=pl.ANY)
    return pl.pallas_call(
        project_kernel,
        in_specs=[pl.BlockSpec(memory_space=pltpu.SMEM)] + [vmem] * 5 + [hbm] * 3,
        out_specs=vmem,
        out_shape=jax.ShapeDtypeStruct((COLS, XS * ROWS, CHUNK_PAD), jnp.bfloat16),
        scratch_shapes=[
            pltpu.VMEM((PIECES, CHUNK_PAD, PIECE), jnp.bfloat16),
            pltpu.SemaphoreType.DMA((PIECES + 24,)),
        ],
        compiler_params=pltpu.CompilerParams(vmem_limit_bytes=40 * 2**20),
        name="project",
    )(place, *tokens, shard, mine, other)


def s_project_kernel(
    place_ref, tokens_ref, own_ref, left_ref, right_ref, far_a_ref, far_b_ref, out_ref, weights
):
    core, y, zh, x = [place_ref[i] for i in range(4)]
    blocks = [(j, zh) for j in range(PIECES)]
    for c in (core, 1 - core):
        for dy in NEAR_Y:
            for dz in NEAR_Z:
                blocks.append((c * 4 + lax.rem(y + dy + 4, 4), lax.rem(zh + dz + 4, 4)))
    for b, dx in enumerate(NEAR_Y):
        xs = lax.rem(x + dx + 4, 4)
        for i, (j, zs) in enumerate(blocks):
            if b < 3:
                block = (own_ref, left_ref, right_ref)[b][i]
            elif i < 16:
                block = far_a_ref[i]
            else:
                block = far_b_ref[i - 16]
            row = (xs * ZS + zs) * S_SHARD
            for half in range(2):
                rows = pl.ds(pl.multiple_of(row + half * S_ROWS, S_ROWS), S_ROWS)
                weights[j, rows, :] = block[:, half * LANES : (half + 1) * LANES]
    for n in range(SW // N_BLOCK):
        part = jnp.concatenate([weights[2 * n], weights[2 * n + 1]], axis=1)
        out_ref[:, n * N_BLOCK : (n + 1) * N_BLOCK] = jnp.dot(
            tokens_ref[...], part, preferred_element_type=jnp.float32
        ).astype(jnp.bfloat16)


def s_project(place, tokens, raw):
    return pl.pallas_call(
        s_project_kernel,
        in_specs=[pl.BlockSpec(memory_space=pltpu.SMEM)]
        + [pl.BlockSpec(memory_space=pltpu.VMEM)] * 6,
        out_shape=jax.ShapeDtypeStruct((TOK, SW), jnp.bfloat16),
        scratch_shapes=[pltpu.VMEM((PIECES, SW, LANES), jnp.bfloat16)],
        compiler_params=pltpu.CompilerParams(vmem_limit_bytes=16 * 2**20),
        name="s_project",
    )(place, tokens, *raw)


HR_GROUPS = CHUNK_PAD // LANES
GROUPS = XS * HR_GROUPS + SW // LANES
BLOCK_OF = {0: 0, 3: 1, 1: 2, 2: 3}


def merge_kernel(
    hr_ref, s_ref, valid_ref, hr_embed_ref, s_embed_ref, hr_gain_ref, s_gain_ref,
    out_ref, mixed_ref,
):
    query = iota2((TOK, TOK), 0)
    key = iota2((TOK, TOK), 1)
    keep = (query % ROWS == key % ROWS) & ((valid_ref[...] > 0) | (query == key))
    bias = jnp.where(keep, 0.0, OFF)
    masks = head_masks(T_HEAD)
    ones = ones_of(masks)

    def merge_group(projected, embed, group):
        joined = (projected + embed.astype(jnp.float32)[:, None, :]).reshape(TOK, LANES)
        joined = joined.astype(jnp.bfloat16)
        mixed = joined.astype(jnp.float32) + attend_group(
            joined, joined, joined, masks, ones, bias, 1.0 / T_HEAD
        )
        mixed_ref[group] = mixed
        return mixed * mixed

    total = jnp.zeros((TOK, LANES), jnp.float32)
    for xs in range(XS):
        for g in range(HR_GROUPS):
            lanes = slice(g * LANES, (g + 1) * LANES)
            part = hr_ref[xs * ZS : (xs + 1) * ZS, :, lanes].astype(jnp.float32)
            part = part.reshape(ZS, XS, ROWS, LANES)
            part = jnp.concatenate(
                [part[:, BLOCK_OF[(x - xs) % XS]] for x in range(XS)], axis=0
            )
            at = slice(xs * CHUNK_PAD + g * LANES, xs * CHUNK_PAD + (g + 1) * LANES)
            total += merge_group(part, hr_embed_ref[:, at], xs * HR_GROUPS + g)
    for n in range(SW // N_BLOCK):
        cols = slice(n * N_BLOCK, (n + 1) * N_BLOCK)
        part = s_ref[:, cols].astype(jnp.float32).reshape(DATES, ROWS, N_BLOCK)
        for g in range(N_BLOCK // LANES):
            lanes = slice(g * LANES, (g + 1) * LANES)
            at = slice(n * N_BLOCK + g * LANES, n * N_BLOCK + (g + 1) * LANES)
            group = XS * HR_GROUPS + n * (N_BLOCK // LANES) + g
            total += merge_group(part[:, :, lanes], s_embed_ref[:, at], group)
    scale = lax.rsqrt(jnp.sum(total, axis=1, keepdims=True) * (1.0 / F) + 1e-06)
    for xs in range(XS):
        for g in range(HR_GROUPS):
            width = min(LANES, CHUNK - g * LANES)
            at = xs * CHUNK_PAD + g * LANES
            value = mixed_ref[xs * HR_GROUPS + g] * scale * hr_gain_ref[:, at : at + LANES]
            to = xs * CHUNK + g * LANES
            out_ref[:, to : to + width] = value[:, :width].astype(jnp.bfloat16)
    for g in range(SW // LANES):
        lanes = slice(g * LANES, (g + 1) * LANES)
        value = mixed_ref[XS * HR_GROUPS + g] * scale * s_gain_ref[:, lanes]
        out_ref[:, HRW + g * LANES : HRW + (g + 1) * LANES] = value.astype(jnp.bfloat16)


def merge(hr, s_out, valid, embed, gain):
    def padded(array):
        array = array[:, :HRW].reshape(-1, XS, CHUNK)
        return jnp.pad(array, ((0, 0), (0, 0), (0, CHUNK_PAD - CHUNK))).reshape(-1, XS * CHUNK_PAD)

    return pl.pallas_call(
        merge_kernel,
        out_shape=jax.ShapeDtypeStruct((TOK, F), jnp.bfloat16),
        scratch_shapes=[pltpu.VMEM((GROUPS, TOK, LANES), jnp.float32)],
        compiler_params=pltpu.CompilerParams(vmem_limit_bytes=40 * 2**20),
        name="merge",
    )(
        hr, s_out, valid, padded(embed), embed[:, HRW:], padded(gain), gain[:, HRW:]
    )


def ring(x, axis, by):
    size = lax.axis_size(axis)
    return lax.ppermute(x, axis, [(i, (i + by) % size) for i in range(size)])


def after(x, *others):
    return lax.optimization_barrier((x,) + others)[0]


def neighbours(x, axis):
    return ring(x, axis, 1), ring(x, axis, -1)


def opposite(pair, axis):
    half = pair[0].shape[0] // 2
    return ring(pair[0][:half], axis, 1), ring(pair[1][half:], axis, -1)


def per_device(hr_qkv, s_qkv, hr_proj, s_proj, shifts, cloud_valid, date_embed, norm_gain):
    half = TOK // 2
    core, y, zh, x = [lax.axis_index(axis) for axis in ("core", "y", "zh", "x")]
    place = jnp.stack([core, y, zh, x]).astype(jnp.int32)
    own = hr_qkv.reshape(3, TOK, HRW)
    below = ring(own[:, :half], SPACE, -1)

    index = core * 4 + y
    shard = hr_proj.T
    s_shard = s_proj.reshape(2, S_ROWS, PIECES, LANES).transpose(2, 1, 0, 3)
    s_shard = s_shard.reshape(PIECES, S_ROWS, 2 * LANES)
    piece = jnp.concatenate(
        [
            lax.dynamic_slice_in_dim(shard, jnp.minimum(index * PIECE, LAST), PIECE, axis=1),
            jnp.pad(s_shard[index], ((0, 0), (0, LANES))),
        ],
        axis=0,
    )
    near = neighbours(piece, "zh")

    tile_out = tile_attention(s_qkv.reshape(3, TOK, SW))
    below = after(below, tile_out, near)
    window_out, passed = window_attention(shifts, own, below)
    above = ring(passed, SPACE, 1)
    near = after(near, window_out)
    foreign = jnp.concatenate(near + opposite(near, "zh"), axis=0)

    window_out = window_out.reshape(COLS, ROWS, HRW)
    top = window_out[:, :MARGIN] + above.reshape(COLS, MARGIN, HRW)
    window_out = jnp.concatenate([top, window_out[:, MARGIN:]], axis=1).reshape(TOK, HRW)
    beside = neighbours(window_out, "x")
    near = after(neighbours(foreign, "y"), beside)
    far = opposite(beside, "x")
    mine = jnp.concatenate((foreign,) + near + opposite(near, "y"), axis=0)
    mine = after(mine, far)
    other = ring(mine, "core", 1)

    s_tokens = lax.all_to_all(
        tile_out.reshape(COLS, ROWS, SW), DATE, split_axis=0, concat_axis=0, tiled=True
    )
    hr_out = project(place, (window_out,) + beside + far, shard, mine, other)
    hr_out = lax.all_to_all(hr_out, DATE, split_axis=0, concat_axis=0, tiled=True)

    raw = [
        part.reshape(-1, PIECE_ROWS, PIECE)[:, SHARD:, : 2 * LANES] for part in (mine, other)
    ]
    raw = jnp.concatenate([s_shard] + raw, axis=0)
    near = neighbours(raw, "x")
    s_out = s_project(place, s_tokens.reshape(TOK, SW), (raw,) + near + opposite(near, "x"))

    out = merge(
        hr_out,
        s_out,
        cloud_valid.reshape(1, TOK),
        date_embed,
        norm_gain.reshape(1, F),
    )
    return out.reshape(DATES, ROWS, 1, F)


def solution(mesh):
    fine = Mesh(mesh.devices.reshape(4, 4, 2, 4, 4), SPACE + DATE)
    in_specs = (
        P(None, DATE, SPACE, None, None),
        P(None, DATE, SPACE, None, None),
        P(None, DATE),
        P(DATE, None),
        P(DATE),
        P(None, SPACE, DATE),
        P(),
        P(),
    )
    out_specs = P(None, SPACE, DATE, None)
    return jax.shard_map(
        per_device, mesh=fine, in_specs=in_specs, out_specs=out_specs, check_vma=False
    )
```

time: 545 us -> 192 us (0.35)
  the two profiles are of different devices: /device:TPU:15 before, /device:TPU:41 now
where the time goes in v2:
time: 192 us; the launch traced here: 190 us
  starting transfers between devices  86.5 us (45%)
  waiting for transfers between devices  64 us (33%)
  local copies, waits for them, and re-layouts  20.5 us (11%)
  Pallas kernels  17.4 us (9%)
    ppermute x19, starting transfers between devices, ring(): return lax.ppermute(x, axis, [(i, (i + by) % size) for i in range(size)])  72.9 us
    ppermute x19, waiting for transfers between devices, ring(): return lax.ppermute(x, axis, [(i, (i + by) % size) for i in range(size)])  47.6 us
    unnamed x53, local copies, waits for them, and re-layouts  12.2 us
    all_to_all x1, waiting for transfers between devices, per_device(): lax.all_to_all(tile_out.reshape(COLS, ROWS, SW), DATE, split_axis=0, conc...  9.87 us
    all_to_all x1, starting transfers between devices, per_device(): lax.all_to_all(tile_out.reshape(COLS, ROWS, SW), DATE, split_axis=0, conc...  9.59 us
    pallas_call x1, Pallas kernels, project(): pl.pallas_call(project_kernel, in_specs=[pl.BlockSpec(memory_space=pltpu....  7.85 us
    all_to_all x1, waiting for transfers between devices, per_device(): lax.all_to_all(hr_out, DATE, split_axis=0, concat_axis=0, tiled=True)  6.52 us
    all_to_all x1, starting transfers between devices, per_device(): lax.all_to_all(hr_out, DATE, split_axis=0, concat_axis=0, tiled=True)  3.96 us
  transfers between devices with their start and end apart: 21, of which 10 were waited for; matrix products, arithmetic and copies ran while one was open for 5% of the time, Pallas kernels for 5%

profile of v2, /device:TPU:41, one launch (start us, length us, event | category | flops | bytes accessed | tf_op | source)
XLA Modules:
  0.0 190.5 jit_solution(5610682756583506998)
XLA Ops:
  0.0 2.5 %slice.68 = bf16[3,64,2816]{2,1,0:T(8,128)(2,1)} slice(bf16[3,128,2816]{2,1,0:T(8,128)(2,1)} %bitcast.34), slice={[0:3], [0:64], [0:2816]} | slice | bytes 2162688 | tf_op jit(solution)/shard_map/slice | solution.py:381
  2.5 2.6 %collective-permute-start = (bf16[3,64,2816]{2,1,0:T(8,128)(2,1)}, bf16[3,64,2816]{2,1,0:T(8,128)(2,1)S(1)}, u32[]{:S(2)}, u32[]{:S(2)}) collective-permute-start(bf16[3,64,2816]{2,1,0:T(8,128)(2,1)} %slice.68), channel_id=1, source_target_pairs={{0,496},{16,0},{32,16},{48,32},{64,48},{80,64},{96,80},{112,96},{1... | collective-permute-start | bytes 3244040 | tf_op jit(solution)/shard_map/ppermute | solution.py:360
  5.1 0.1 copy.19
  5.2 0.1 reshape.57
  5.3 1.0 dynamic-slice_bitcast_fusion
  6.4 8.8 %collective-permute-start.1 = (bf16[208,384]{1,0:T(8,128)(2,1)S(1)}, bf16[208,384]{1,0:T(8,128)(2,1)S(1)}, u32[]{:S(2)}, u32[]{:S(2)}) collective-permute-start(bf16[208,384]{1,0:T(8,128)(2,1)S(1)} %fusion.1), channel_id=1, source_target_pairs={{0,1},{1,2},{2,3},{3,0},{4,5},{5,6},{6,7},{7,4},{8,9},{9,10},{10,1... | collective-permute-start | bytes 479240 | tf_op jit(solution)/shard_map/ppermute | solution.py:360
  15.2 4.7 %collective-permute-start.2 = (bf16[208,384]{1,0:T(8,128)(2,1)S(1)}, bf16[208,384]{1,0:T(8,128)(2,1)S(1)}, u32[]{:S(2)}, u32[]{:S(2)}) collective-permute-start(bf16[208,384]{1,0:T(8,128)(2,1)S(1)} %fusion.1), channel_id=1, source_target_pairs={{0,3},{1,0},{2,1},{3,2},{4,7},{5,4},{6,5},{7,6},{8,11},{9,8},{10,9... | collective-permute-start | bytes 479240 | tf_op jit(solution)/shard_map/ppermute | solution.py:360
  20.6 1.1 copy-done.5
  21.7 0.9 tile_attention.1
  22.6 0.7 copy-done.4
  23.3 16.9 %collective-permute-done.1 = bf16[208,384]{1,0:T(8,128)(2,1)S(1)} collective-permute-done((bf16[208,384]{1,0:T(8,128)(2,1)S(1)}, bf16[208,384]{1,0:T(8,128)(2,1)S(1)}, u32[]{:S(2)}, u32[]{:S(2)}) %collective-permute-start.1) | collective-permute-done | bytes 159776 | tf_op jit(solution)/shard_map/ppermute | solution.py:360
  40.2 3.7 %window_attention.1 = (bf16[128,2816]{1,0:T(8,128)(2,1)S(1)}, bf16[64,2816]{1,0:T(8,128)(2,1)S(1)}) custom-call(s32[1]{0:T(128)S(6)} %copy.30.offset_ref, bf16[3,128,2816]{2,1,0:T(8,128)(2,1)S(1)} %bitcast.35, bf16[3,64,2816]{2,1,0:T(8,128)(2,1)S(1)} %collective-permute-done.below_ref), custom_call_target="tpu_custom_call" | custom-call | tf_op jit(solution)/shard_map/window_attention/pallas_call | solution.py:114
  44.0 0.8 copy-done.6
  44.9 6.5 %collective-permute-start.3 = (bf16[64,2816]{1,0:T(8,128)(2,1)S(1)}, bf16[64,2816]{1,0:T(8,128)(2,1)S(1)}, u32[]{:S(2)}, u32[]{:S(2)}) collective-permute-start(bf16[64,2816]{1,0:T(8,128)(2,1)S(1)} %get-tuple-element.15), channel_id=1, source_target_pairs={{0,16},{16,32},{32,48},{48,64},{64,80},{80,96},{96,112},{112,128},... | collective-permute-start | bytes 1081352 | tf_op jit(solution)/shard_map/ppermute | solution.py:360
  51.4 0.6 slice.56
  52.0 3.2 %collective-permute-start.8 = (bf16[104,384]{1,0:T(8,128)(2,1)}, bf16[104,384]{1,0:T(8,128)(2,1)}, u32[]{:S(2)}, u32[]{:S(2)}) collective-permute-start(bf16[104,384]{1,0:T(8,128)(2,1)} %slice.56), channel_id=1, source_target_pairs={{0,1},{1,2},{2,3},{3,0},{4,5},{5,6},{6,7},{7,4},{8,9},{9,10},{10,1... | collective-permute-start | bytes 239624 | tf_op jit(solution)/shard_map/ppermute | solution.py:360
  55.3 0.6 slice.57
  55.9 6.0 %collective-permute-start.9 = (bf16[104,384]{1,0:T(8,128)(2,1)}, bf16[104,384]{1,0:T(8,128)(2,1)}, u32[]{:S(2)}, u32[]{:S(2)}) collective-permute-start(bf16[104,384]{1,0:T(8,128)(2,1)} %slice.57), channel_id=1, source_target_pairs={{0,3},{1,0},{2,1},{3,2},{4,7},{5,4},{6,5},{7,6},{8,11},{9,8},{10,9... | collective-permute-start | bytes 239624 | tf_op jit(solution)/shard_map/ppermute | solution.py:360
  61.9 0.7 constant_dynamic-update-slice_fusion.3
  62.6 0.1 reshape.59
  62.7 0.4 slice_add_fusion
  63.1 0.4 maximum_bitcast_fusion.own_ref
  63.4 3.1 %collective-permute-start.4 = (bf16[128,2816]{1,0:T(8,128)(2,1)S(1)}, bf16[128,2816]{1,0:T(8,128)(2,1)S(1)}, u32[]{:S(2)}, u32[]{:S(2)}) collective-permute-start(bf16[128,2816]{1,0:T(8,128)(2,1)S(1)} %maximum_bitcast_fusion.own_ref), channel_id=1, source_target_pairs={{0,4},{4,8},{8,12},{12,0},{1,5},{5,9},{9,13},{13,1},{2,6},{6,10},{... | collective-permute-start | bytes 2162696 | tf_op jit(solution)/shard_map/ppermute | solution.py:360
  66.5 3.4 %collective-permute-start.5 = (bf16[128,2816]{1,0:T(8,128)(2,1)S(1)}, bf16[128,2816]{1,0:T(8,128)(2,1)S(1)}, u32[]{:S(2)}, u32[]{:S(2)}) collective-permute-start(bf16[128,2816]{1,0:T(8,128)(2,1)S(1)} %maximum_bitcast_fusion.own_ref), channel_id=1, source_target_pairs={{0,12},{4,0},{8,4},{12,8},{1,13},{5,1},{9,5},{13,9},{2,14},{6,2},{... | collective-permute-start | bytes 2162696 | tf_op jit(solution)/shard_map/ppermute | solution.py:360
  70.0 0.9 constant_dynamic-update-slice_fusion.1
  70.9 0.9 constant_dynamic-update-slice_fusion
  71.9 3.2 %collective-permute-start.10 = (bf16[624,384]{1,0:T(8,128)(2,1)S(1)}, bf16[624,384]{1,0:T(8,128)(2,1)S(1)}, u32[]{:S(2)}, u32[]{:S(2)}) collective-permute-start(bf16[624,384]{1,0:T(8,128)(2,1)S(1)} %get-tuple-element.27), channel_id=1, source_target_pairs={{0,128},{128,256},{256,384},{384,0},{1,129},{129,257},{257,385},{3... | collective-permute-start | bytes 1437704 | tf_op jit(solution)/shard_map/ppermute | solution.py:360
  75.1 2.1 %collective-permute-start.11 = (bf16[624,384]{1,0:T(8,128)(2,1)S(1)}, bf16[624,384]{1,0:T(8,128)(2,1)S(1)}, u32[]{:S(2)}, u32[]{:S(2)}) collective-permute-start(bf16[624,384]{1,0:T(8,128)(2,1)S(1)} %get-tuple-element.27), channel_id=1, source_target_pairs={{0,384},{128,0},{256,128},{384,256},{1,385},{129,1},{257,129},{385... | collective-permute-start | bytes 1437704 | tf_op jit(solution)/shard_map/ppermute | solution.py:360
  77.2 4.2 %collective-permute-done.4.left_ref = bf16[128,2816]{1,0:T(8,128)(2,1)S(1)} collective-permute-done((bf16[128,2816]{1,0:T(8,128)(2,1)S(1)}, bf16[128,2816]{1,0:T(8,128)(2,1)S(1)}, u32[]{:S(2)}, u32[]{:S(2)}) %collective-permute-start.4) | collective-permute-done | bytes 720928 | tf_op jit(solution)/shard_map/ppermute | solution.py:360
  81.4 2.2 %collective-permute-start.6 = (bf16[64,2816]{1,0:T(8,128)(2,1)S(1)}, bf16[64,2816]{1,0:T(8,128)(2,1)S(1)}, u32[]{:S(2)}, u32[]{:S(2)}) collective-permute-start(bf16[64,2816]{1,0:T(8,128)(2,1)S(1)} %slice.71), channel_id=1, source_target_pairs={{0,4},{4,8},{8,12},{12,0},{1,5},{5,9},{9,13},{13,1},{2,6},{6,10},{... | collective-permute-start | bytes 1081352 | tf_op jit(solution)/shard_map/ppermute | solution.py:360
  83.6 0.3 collective-permute-done.5.right_ref
  83.9 4.3 %collective-permute-start.7 = (bf16[64,2816]{1,0:T(8,128)(2,1)S(1)}, bf16[64,2816]{1,0:T(8,128)(2,1)S(1)}, u32[]{:S(2)}, u32[]{:S(2)}) collective-permute-start(bf16[64,2816]{1,0:T(8,128)(2,1)S(1)} %slice.72), channel_id=1, source_target_pairs={{0,12},{4,0},{8,4},{12,8},{1,13},{5,1},{9,5},{13,9},{2,14},{6,2},{... | collective-permute-start | bytes 1081352 | tf_op jit(solution)/shard_map/ppermute | solution.py:360
  88.3 3.3 %collective-permute-start.12 = (bf16[312,384]{1,0:T(8,128)(2,1)S(1)}, bf16[312,384]{1,0:T(8,128)(2,1)S(1)}, u32[]{:S(2)}, u32[]{:S(2)}) collective-permute-start(bf16[312,384]{1,0:T(8,128)(2,1)S(1)} %slice.58), channel_id=1, source_target_pairs={{0,128},{128,256},{256,384},{384,0},{1,129},{129,257},{257,385},{3... | collective-permute-start | bytes 718856 | tf_op jit(solution)/shard_map/ppermute | solution.py:360
  91.7 3.6 %collective-permute-start.13 = (bf16[312,384]{1,0:T(8,128)(2,1)S(1)}, bf16[312,384]{1,0:T(8,128)(2,1)S(1)}, u32[]{:S(2)}, u32[]{:S(2)}) collective-permute-start(bf16[312,384]{1,0:T(8,128)(2,1)S(1)} %slice.59), channel_id=1, source_target_pairs={{0,384},{128,0},{256,128},{384,256},{1,385},{129,1},{257,129},{385... | collective-permute-start | bytes 718856 | tf_op jit(solution)/shard_map/ppermute | solution.py:360
  95.5 4.2 %collective-permute-done.12 = bf16[312,384]{1,0:T(8,128)(2,1)S(1)} collective-permute-done((bf16[312,384]{1,0:T(8,128)(2,1)S(1)}, bf16[312,384]{1,0:T(8,128)(2,1)S(1)}, u32[]{:S(2)}, u32[]{:S(2)}) %collective-permute-start.12) | collective-permute-done | bytes 239648 | tf_op jit(solution)/shard_map/ppermute | solution.py:360
  99.7 2.7 %collective-permute-done.13 = bf16[312,384]{1,0:T(8,128)(2,1)S(1)} collective-permute-done((bf16[312,384]{1,0:T(8,128)(2,1)S(1)}, bf16[312,384]{1,0:T(8,128)(2,1)S(1)}, u32[]{:S(2)}, u32[]{:S(2)}) %collective-permute-start.13) | collective-permute-done | bytes 239648 | tf_op jit(solution)/shard_map/ppermute | solution.py:360
  102.5 0.7 copy-done.8
  103.2 0.8 copy-done.10
  104.0 2.8 %collective-permute-start.14 = (bf16[2496,384]{1,0:T(8,128)(2,1)S(1)}, bf16[2496,384]{1,0:T(8,128)(2,1)}, u32[]{:S(2)}, u32[]{:S(2)}) collective-permute-start(bf16[2496,384]{1,0:T(8,128)(2,1)S(1)} %constant_dynamic-update-slice_fusion.4.mine_ref), channel_id=1, source_target_pairs={{0,16},{16,0},{1,17},{17,1},{2,18},{18,2},{3,19},{19,3},{4,20},{20... | collective-permute-start | bytes 5750792 | tf_op jit(solution)/shard_map/ppermute | solution.py:360
  106.8 9.6 %all-to-all-start.1 = ((bf16[16,8,1024]{2,1,0:T(8,128)(2,1)}), bf16[16,8,1024]{2,1,0:T(8,128)(2,1)}, u32[]{:S(2)}, u32[]{:S(2)}) async-start(bf16[16,8,1024]{2,1,0:T(8,128)(2,1)} %bitcast.38), calls=%async_computation.1 | async-start | bytes 524288 | tf_op jit(solution)/shard_map/all_to_all | solution.py:413
  116.5 1.1 copy-done.2
  117.6 1.2 copy-done.3
  118.8 1.0 copy-done.9
  119.8 1.0 copy-done.11
  120.7 7.8 %project.1 = bf16[16,32,768]{2,1,0:T(8,128)(2,1)} custom-call(s32[4]{0:T(128)S(1)} %pad_add_fusion.place_ref, bf16[128,2816]{1,0:T(8,128)(2,1)S(1)} %maximum_bitcast_fusion.own_ref, bf16[128,2816]{1,0:T(8,128)(2,1)S(1)} %collective-permute-done.4.left_ref, bf16[128,2816]{1,0:T(8,128)(2,1)S(1)} %copy-done.2, bf16[64,2816]{1,0:T(8,128)(2,1)S(1)} %copy-done.9, ...), custom_call_target="tpu_custom_call" | custom-call | tf_op jit(solution)/shard_map/project/pallas_call | solution.py:229
  128.6 9.9 %all-to-all-done.1 = bf16[16,8,1024]{2,1,0:T(8,128)(2,1)} async-done(((bf16[16,8,1024]{2,1,0:T(8,128)(2,1)}), bf16[16,8,1024]{2,1,0:T(8,128)(2,1)}, u32[]{:S(2)}, u32[]{:S(2)}) %all-to-all-start.1) | async-done | bytes 262176 | tf_op jit(solution)/shard_map/all_to_all | solution.py:413
  138.5 4.0 %all-to-all-start = ((bf16[16,32,768]{2,1,0:T(8,128)(2,1)}), bf16[16,32,768]{2,1,0:T(8,128)(2,1)S(1)}, u32[]{:S(2)}, u32[]{:S(2)}) async-start(bf16[16,32,768]{2,1,0:T(8,128)(2,1)} %project.1), calls=%async_computation | async-start | bytes 1572864 | tf_op jit(solution)/shard_map/all_to_all | solution.py:417
  142.5 1.0 slice.74
  143.6 3.3 %collective-permute-start.15 = (bf16[32,32,256]{2,1,0:T(8,128)(2,1)S(1)}, bf16[32,32,256]{2,1,0:T(8,128)(2,1)S(1)}, u32[]{:S(2)}, u32[]{:S(2)}) collective-permute-start(bf16[32,32,256]{2,1,0:T(8,128)(2,1)S(1)} %pad_maximum_fusion.own_ref), channel_id=1, source_target_pairs={{0,4},{4,8},{8,12},{12,0},{1,5},{5,9},{9,13},{13,1},{2,6},{6,10},{... | collective-permute-start | bytes 1572872 | tf_op jit(solution)/shard_map/ppermute | solution.py:360
  146.9 3.2 %collective-permute-start.16 = (bf16[32,32,256]{2,1,0:T(8,128)(2,1)S(1)}, bf16[32,32,256]{2,1,0:T(8,128)(2,1)S(1)}, u32[]{:S(2)}, u32[]{:S(2)}) collective-permute-start(bf16[32,32,256]{2,1,0:T(8,128)(2,1)S(1)} %pad_maximum_fusion.own_ref), channel_id=1, source_target_pairs={{0,12},{4,0},{8,4},{12,8},{1,13},{5,1},{9,5},{13,9},{2,14},{6,2},{... | collective-permute-start | bytes 1572872 | tf_op jit(solution)/shard_map/ppermute | solution.py:360
  150.1 9.4 %collective-permute-done.15.left_ref = bf16[32,32,256]{2,1,0:T(8,128)(2,1)S(1)} collective-permute-done((bf16[32,32,256]{2,1,0:T(8,128)(2,1)S(1)}, bf16[32,32,256]{2,1,0:T(8,128)(2,1)S(1)}, u32[]{:S(2)}, u32[]{:S(2)}) %collective-permute-start.15) | collective-permute-done | bytes 524320 | tf_op jit(solution)/shard_map/ppermute | solution.py:360
  159.5 1.9 %collective-permute-start.17 = (bf16[16,32,256]{2,1,0:T(8,128)(2,1)S(1)}, bf16[16,32,256]{2,1,0:T(8,128)(2,1)S(1)}, u32[]{:S(2)}, u32[]{:S(2)}) collective-permute-start(bf16[16,32,256]{2,1,0:T(8,128)(2,1)S(1)} %slice.75), channel_id=1, source_target_pairs={{0,4},{4,8},{8,12},{12,0},{1,5},{5,9},{9,13},{13,1},{2,6},{6,10},{... | collective-permute-start | bytes 786440 | tf_op jit(solution)/shard_map/ppermute | solution.py:360
  161.5 0.7 slice.76
  162.2 4.7 %collective-permute-start.18 = (bf16[16,32,256]{2,1,0:T(8,128)(2,1)}, bf16[16,32,256]{2,1,0:T(8,128)(2,1)S(1)}, u32[]{:S(2)}, u32[]{:S(2)}) collective-permute-start(bf16[16,32,256]{2,1,0:T(8,128)(2,1)} %slice.76), channel_id=1, source_target_pairs={{0,12},{4,0},{8,4},{12,8},{1,13},{5,1},{9,5},{13,9},{2,14},{6,2},{... | collective-permute-start | bytes 786440 | tf_op jit(solution)/shard_map/ppermute | solution.py:360
  167.1 0.1 reshape.65.valid_ref
  167.2 0.1 reshape.66
  167.5 0.1 reshape.69
  167.6 1.2 collective-permute-done.17.far_a_ref
  168.8 8.6 %collective-permute-done.18.far_b_ref = bf16[16,32,256]{2,1,0:T(8,128)(2,1)S(1)} collective-permute-done((bf16[16,32,256]{2,1,0:T(8,128)(2,1)}, bf16[16,32,256]{2,1,0:T(8,128)(2,1)S(1)}, u32[]{:S(2)}, u32[]{:S(2)}) %collective-permute-start.18) | collective-permute-done | bytes 262176 | tf_op jit(solution)/shard_map/ppermute | solution.py:360
  177.4 0.7 copy-done.12
  178.1 0.9 copy-done.13
  179.0 1.7 s_project.1.s_ref
  180.8 6.5 %all-to-all-done.hr_ref = bf16[16,32,768]{2,1,0:T(8,128)(2,1)S(1)} async-done(((bf16[16,32,768]{2,1,0:T(8,128)(2,1)}), bf16[16,32,768]{2,1,0:T(8,128)(2,1)S(1)}, u32[]{:S(2)}, u32[]{:S(2)}) %all-to-all-start) | async-done | bytes 786464 | tf_op jit(solution)/shard_map/all_to_all | solution.py:417
  187.3 3.2 %merge.1 = bf16[128,3840]{1,0:T(8,128)(2,1)} custom-call(bf16[16,32,768]{2,1,0:T(8,128)(2,1)S(1)} %all-to-all-done.hr_ref, bf16[128,1024]{1,0:T(8,128)(2,1)S(1)} %s_project.1.s_ref, s32[1,128]{1,0:T(1,128)S(1)} %reshape.65.valid_ref, bf16[16,3072]{1,0:T(8,128)(2,1)S(1)} %bitcast.41, bf16[16,1024]{1,0:T(8,128)(2,1)S(1)} %slice.65.s_embed_ref, ...), custom_call_target="tpu_custom_call" | custom-call | tf_op jit(solution)/shard_map/merge/pallas_call | solution.py:347
  (69 shorter events, 0.9 us)
Async XLA Ops:
  0.0 5.0 %copy-start.17 = (bf16[64,1024]{1,0:T(8,128)(2,1)S(1)}, bf16[64,1024]{1,0:T(8,128)(2,1)}, u32[]{:S(2)}) copy-start(bf16[64,1024]{1,0:T(8,128)(2,1)} %param.11) | copy-start | bytes 393220
  0.0 40.2 %copy-start = (bf16[3,1,8,16,2816]{4,3,2,1,0:T(8,128)(2,1)S(1)}, bf16[3,1,8,16,2816]{4,3,2,1,0:T(8,128)(2,1)}, u32[]{:S(2)}) copy-start(bf16[3,1,8,16,2816]{4,3,2,1,0:T(8,128)(2,1)} %param.8) | copy-start | bytes 6488068
  2.5 37.8 %collective-permute-start = (bf16[3,64,2816]{2,1,0:T(8,128)(2,1)}, bf16[3,64,2816]{2,1,0:T(8,128)(2,1)S(1)}, u32[]{:S(2)}, u32[]{:S(2)}) collective-permute-start(bf16[3,64,2816]{2,1,0:T(8,128)(2,1)} %slice.68), channel_id=1, source_target_pairs={{0,496},{16,0},{32,16},{48,32},{64,48},{80,64},{96,80},{112,96},{1... | collective-permute-start | bytes 3244040 | tf_op jit(solution)/shard_map/ppermute | solution.py:360
  6.4 33.8 %collective-permute-start.1 = (bf16[208,384]{1,0:T(8,128)(2,1)S(1)}, bf16[208,384]{1,0:T(8,128)(2,1)S(1)}, u32[]{:S(2)}, u32[]{:S(2)}) collective-permute-start(bf16[208,384]{1,0:T(8,128)(2,1)S(1)} %fusion.1), channel_id=1, source_target_pairs={{0,1},{1,2},{2,3},{3,0},{4,5},{5,6},{6,7},{7,4},{8,9},{9,10},{10,1... | collective-permute-start | bytes 479240 | tf_op jit(solution)/shard_map/ppermute | solution.py:360
  15.2 25.0 %collective-permute-start.2 = (bf16[208,384]{1,0:T(8,128)(2,1)S(1)}, bf16[208,384]{1,0:T(8,128)(2,1)S(1)}, u32[]{:S(2)}, u32[]{:S(2)}) collective-permute-start(bf16[208,384]{1,0:T(8,128)(2,1)S(1)} %fusion.1), channel_id=1, source_target_pairs={{0,3},{1,0},{2,1},{3,2},{4,7},{5,4},{6,5},{7,6},{8,11},{9,8},{10,9... | collective-permute-start | bytes 479240 | tf_op jit(solution)/shard_map/ppermute | solution.py:360
  20.6 1.1 copy-start.5
  22.5 0.7 copy-start.4
  40.2 22.3 %copy-start.15 = (bf16[208,384]{1,0:T(8,128)(2,1)}, bf16[208,384]{1,0:T(8,128)(2,1)S(1)}, u32[]{:S(2)}) copy-start(bf16[208,384]{1,0:T(8,128)(2,1)S(1)} %collective-permute-done.2) | copy-start | bytes 479236
  44.0 0.9 copy-start.6
  44.8 17.8 %copy-start.7 = (bf16[128,2816]{1,0:T(8,128)(2,1)S(1)}, bf16[128,2816]{1,0:T(8,128)(2,1)}, u32[]{:S(2)}) copy-start(bf16[128,2816]{1,0:T(8,128)(2,1)} %copy-done.6) | copy-start | bytes 2162692
  44.9 17.7 %collective-permute-start.3 = (bf16[64,2816]{1,0:T(8,128)(2,1)S(1)}, bf16[64,2816]{1,0:T(8,128)(2,1)S(1)}, u32[]{:S(2)}, u32[]{:S(2)}) collective-permute-start(bf16[64,2816]{1,0:T(8,128)(2,1)S(1)} %get-tuple-element.15), channel_id=1, source_target_pairs={{0,16},{16,32},{32,48},{48,64},{64,80},{80,96},{96,112},{112,128},... | collective-permute-start | bytes 1081352 | tf_op jit(solution)/shard_map/ppermute | solution.py:360
  52.0 18.0 %collective-permute-start.8 = (bf16[104,384]{1,0:T(8,128)(2,1)}, bf16[104,384]{1,0:T(8,128)(2,1)}, u32[]{:S(2)}, u32[]{:S(2)}) collective-permute-start(bf16[104,384]{1,0:T(8,128)(2,1)} %slice.56), channel_id=1, source_target_pairs={{0,1},{1,2},{2,3},{3,0},{4,5},{5,6},{6,7},{7,4},{8,9},{9,10},{10,1... | collective-permute-start | bytes 239624 | tf_op jit(solution)/shard_map/ppermute | solution.py:360
  55.9 15.0 %collective-permute-start.9 = (bf16[104,384]{1,0:T(8,128)(2,1)}, bf16[104,384]{1,0:T(8,128)(2,1)}, u32[]{:S(2)}, u32[]{:S(2)}) collective-permute-start(bf16[104,384]{1,0:T(8,128)(2,1)} %slice.57), channel_id=1, source_target_pairs={{0,3},{1,0},{2,1},{3,2},{4,7},{5,4},{6,5},{7,6},{8,11},{9,8},{10,9... | collective-permute-start | bytes 239624 | tf_op jit(solution)/shard_map/ppermute | solution.py:360
  62.7 7.3 %copy-start.16 = (bf16[208,384]{1,0:T(8,128)(2,1)S(1)}, bf16[208,384]{1,0:T(8,128)(2,1)}, u32[]{:S(2)}) copy-start(bf16[208,384]{1,0:T(8,128)(2,1)} %copy-done.15) | copy-start | bytes 479236
  62.7 7.3 %copy-start.18 = (bf16[624,384]{1,0:T(8,128)(2,1)S(1)}, bf16[624,384]{1,0:T(8,128)(2,1)}, u32[]{:S(2)}) copy-start(bf16[624,384]{1,0:T(8,128)(2,1)} %get-tuple-element.25) | copy-start | bytes 1437700
  63.4 18.0 %collective-permute-start.4 = (bf16[128,2816]{1,0:T(8,128)(2,1)S(1)}, bf16[128,2816]{1,0:T(8,128)(2,1)S(1)}, u32[]{:S(2)}, u32[]{:S(2)}) collective-permute-start(bf16[128,2816]{1,0:T(8,128)(2,1)S(1)} %maximum_bitcast_fusion.own_ref), channel_id=1, source_target_pairs={{0,4},{4,8},{8,12},{12,0},{1,5},{5,9},{9,13},{13,1},{2,6},{6,10},{... | collective-permute-start | bytes 2162696 | tf_op jit(solution)/shard_map/ppermute | solution.py:360
  66.5 17.3 %collective-permute-start.5 = (bf16[128,2816]{1,0:T(8,128)(2,1)S(1)}, bf16[128,2816]{1,0:T(8,128)(2,1)S(1)}, u32[]{:S(2)}, u32[]{:S(2)}) collective-permute-start(bf16[128,2816]{1,0:T(8,128)(2,1)S(1)} %maximum_bitcast_fusion.own_ref), channel_id=1, source_target_pairs={{0,12},{4,0},{8,4},{12,8},{1,13},{5,1},{9,5},{13,9},{2,14},{6,2},{... | collective-permute-start | bytes 2162696 | tf_op jit(solution)/shard_map/ppermute | solution.py:360
  71.9 16.4 %collective-permute-start.10 = (bf16[624,384]{1,0:T(8,128)(2,1)S(1)}, bf16[624,384]{1,0:T(8,128)(2,1)S(1)}, u32[]{:S(2)}, u32[]{:S(2)}) collective-permute-start(bf16[624,384]{1,0:T(8,128)(2,1)S(1)} %get-tuple-element.27), channel_id=1, source_target_pairs={{0,128},{128,256},{256,384},{384,0},{1,129},{129,257},{257,385},{3... | collective-permute-start | bytes 1437704 | tf_op jit(solution)/shard_map/ppermute | solution.py:360
  75.1 13.2 %collective-permute-start.11 = (bf16[624,384]{1,0:T(8,128)(2,1)S(1)}, bf16[624,384]{1,0:T(8,128)(2,1)S(1)}, u32[]{:S(2)}, u32[]{:S(2)}) collective-permute-start(bf16[624,384]{1,0:T(8,128)(2,1)S(1)} %get-tuple-element.27), channel_id=1, source_target_pairs={{0,384},{128,0},{256,128},{384,256},{1,385},{129,1},{257,129},{385... | collective-permute-start | bytes 1437704 | tf_op jit(solution)/shard_map/ppermute | solution.py:360
  81.4 21.1 %collective-permute-start.6 = (bf16[64,2816]{1,0:T(8,128)(2,1)S(1)}, bf16[64,2816]{1,0:T(8,128)(2,1)S(1)}, u32[]{:S(2)}, u32[]{:S(2)}) collective-permute-start(bf16[64,2816]{1,0:T(8,128)(2,1)S(1)} %slice.71), channel_id=1, source_target_pairs={{0,4},{4,8},{8,12},{12,0},{1,5},{5,9},{9,13},{13,1},{2,6},{6,10},{... | collective-permute-start | bytes 1081352 | tf_op jit(solution)/shard_map/ppermute | solution.py:360
  83.9 15.8 %copy-start.1 = (bf16[128,2816]{1,0:T(8,128)(2,1)}, bf16[128,2816]{1,0:T(8,128)(2,1)S(1)}, u32[]{:S(2)}) copy-start(bf16[128,2816]{1,0:T(8,128)(2,1)S(1)} %collective-permute-done.5.right_ref) | copy-start | bytes 2162692
  83.9 19.3 %collective-permute-start.7 = (bf16[64,2816]{1,0:T(8,128)(2,1)S(1)}, bf16[64,2816]{1,0:T(8,128)(2,1)S(1)}, u32[]{:S(2)}, u32[]{:S(2)}) collective-permute-start(bf16[64,2816]{1,0:T(8,128)(2,1)S(1)} %slice.72), channel_id=1, source_target_pairs={{0,12},{4,0},{8,4},{12,8},{1,13},{5,1},{9,5},{13,9},{2,14},{6,2},{... | collective-permute-start | bytes 1081352 | tf_op jit(solution)/shard_map/ppermute | solution.py:360
  88.3 11.4 %collective-permute-start.12 = (bf16[312,384]{1,0:T(8,128)(2,1)S(1)}, bf16[312,384]{1,0:T(8,128)(2,1)S(1)}, u32[]{:S(2)}, u32[]{:S(2)}) collective-permute-start(bf16[312,384]{1,0:T(8,128)(2,1)S(1)} %slice.58), channel_id=1, source_target_pairs={{0,128},{128,256},{256,384},{384,0},{1,129},{129,257},{257,385},{3... | collective-permute-start | bytes 718856 | tf_op jit(solution)/shard_map/ppermute | solution.py:360
  91.7 10.8 %collective-permute-start.13 = (bf16[312,384]{1,0:T(8,128)(2,1)S(1)}, bf16[312,384]{1,0:T(8,128)(2,1)S(1)}, u32[]{:S(2)}, u32[]{:S(2)}) collective-permute-start(bf16[312,384]{1,0:T(8,128)(2,1)S(1)} %slice.59), channel_id=1, source_target_pairs={{0,384},{128,0},{256,128},{384,256},{1,385},{129,1},{257,129},{385... | collective-permute-start | bytes 718856 | tf_op jit(solution)/shard_map/ppermute | solution.py:360
  102.5 0.7 copy-start.8
  103.2 0.8 copy-start.10
  104.0 12.5 %collective-permute-start.14 = (bf16[2496,384]{1,0:T(8,128)(2,1)S(1)}, bf16[2496,384]{1,0:T(8,128)(2,1)}, u32[]{:S(2)}, u32[]{:S(2)}) collective-permute-start(bf16[2496,384]{1,0:T(8,128)(2,1)S(1)} %constant_dynamic-update-slice_fusion.4.mine_ref), channel_id=1, source_target_pairs={{0,16},{16,0},{1,17},{17,1},{2,18},{18,2},{3,19},{19,3},{4,20},{20... | collective-permute-start | bytes 5750792 | tf_op jit(solution)/shard_map/ppermute | solution.py:360
  106.8 31.7 %all-to-all-start.1 = ((bf16[16,8,1024]{2,1,0:T(8,128)(2,1)}), bf16[16,8,1024]{2,1,0:T(8,128)(2,1)}, u32[]{:S(2)}, u32[]{:S(2)}) async-start(bf16[16,8,1024]{2,1,0:T(8,128)(2,1)} %bitcast.38), calls=%async_computation.1 | async-start | bytes 524288 | tf_op jit(solution)/shard_map/all_to_all | solution.py:413
  116.5 1.1 copy-start.2
  117.6 1.2 copy-start.3
  118.8 1.0 copy-start.9
  119.8 1.0 copy-start.11
  138.5 48.8 %all-to-all-start = ((bf16[16,32,768]{2,1,0:T(8,128)(2,1)}), bf16[16,32,768]{2,1,0:T(8,128)(2,1)S(1)}, u32[]{:S(2)}, u32[]{:S(2)}) async-start(bf16[16,32,768]{2,1,0:T(8,128)(2,1)} %project.1), calls=%async_computation | async-start | bytes 1572864 | tf_op jit(solution)/shard_map/all_to_all | solution.py:417
  142.4 24.5 %copy-start.14 = (bf16[16,3840]{1,0:T(8,128)(2,1)S(1)}, bf16[16,3840]{1,0:T(8,128)(2,1)}, u32[]{:S(2)}) copy-start(bf16[16,3840]{1,0:T(8,128)(2,1)} %param.14) | copy-start | bytes 368644
  142.5 24.5 %copy-start.20 = (s32[16,8,1]{0,2,1:T(1,128)S(1)}, s32[16,8,1]{0,2,1:T(1,128)}, u32[]{:S(2)}) copy-start(s32[16,8,1]{0,2,1:T(1,128)} %param.13) | copy-start | bytes 1540
  142.5 24.7 %slice-start = ((bf16[16,3840]{1,0:T(8,128)(2,1)}), bf16[16,2816]{1,0:T(8,128)(2,1)S(1)}, s32[]{:S(2)}) async-start(bf16[16,3840]{1,0:T(8,128)(2,1)} %param.14), calls=%async_computation.2 | async-start | bytes 180224 | tf_op jit(solution)/shard_map/slice | solution.py:344
  142.5 24.9 %copy-start.19 = (f32[3840]{0:T(1024)S(1)}, f32[3840]{0:T(1024)}, u32[]{:S(2)}) copy-start(f32[3840]{0:T(1024)} %param.15) | copy-start | bytes 46084
  143.6 15.9 %collective-permute-start.15 = (bf16[32,32,256]{2,1,0:T(8,128)(2,1)S(1)}, bf16[32,32,256]{2,1,0:T(8,128)(2,1)S(1)}, u32[]{:S(2)}, u32[]{:S(2)}) collective-permute-start(bf16[32,32,256]{2,1,0:T(8,128)(2,1)S(1)} %pad_maximum_fusion.own_ref), channel_id=1, source_target_pairs={{0,4},{4,8},{8,12},{12,0},{1,5},{5,9},{9,13},{13,1},{2,6},{6,10},{... | collective-permute-start | bytes 1572872 | tf_op jit(solution)/shard_map/ppermute | solution.py:360
  146.9 14.6 %collective-permute-start.16 = (bf16[32,32,256]{2,1,0:T(8,128)(2,1)S(1)}, bf16[32,32,256]{2,1,0:T(8,128)(2,1)S(1)}, u32[]{:S(2)}, u32[]{:S(2)}) collective-permute-start(bf16[32,32,256]{2,1,0:T(8,128)(2,1)S(1)} %pad_maximum_fusion.own_ref), channel_id=1, source_target_pairs={{0,12},{4,0},{8,4},{12,8},{1,13},{5,1},{9,5},{13,9},{2,14},{6,2},{... | collective-permute-start | bytes 1572872 | tf_op jit(solution)/shard_map/ppermute | solution.py:360
  159.5 9.2 %collective-permute-start.17 = (bf16[16,32,256]{2,1,0:T(8,128)(2,1)S(1)}, bf16[16,32,256]{2,1,0:T(8,128)(2,1)S(1)}, u32[]{:S(2)}, u32[]{:S(2)}) collective-permute-start(bf16[16,32,256]{2,1,0:T(8,128)(2,1)S(1)} %slice.75), channel_id=1, source_target_pairs={{0,4},{4,8},{8,12},{12,0},{1,5},{5,9},{9,13},{13,1},{2,6},{6,10},{... | collective-permute-start | bytes 786440 | tf_op jit(solution)/shard_map/ppermute | solution.py:360
  162.2 15.2 %collective-permute-start.18 = (bf16[16,32,256]{2,1,0:T(8,128)(2,1)}, bf16[16,32,256]{2,1,0:T(8,128)(2,1)S(1)}, u32[]{:S(2)}, u32[]{:S(2)}) collective-permute-start(bf16[16,32,256]{2,1,0:T(8,128)(2,1)} %slice.76), channel_id=1, source_target_pairs={{0,12},{4,0},{8,4},{12,8},{1,13},{5,1},{9,5},{13,9},{2,14},{6,2},{... | collective-permute-start | bytes 786440 | tf_op jit(solution)/shard_map/ppermute | solution.py:360
  177.4 0.7 copy-start.12
  178.1 0.9 copy-start.13

commit v3 on v2

--- a/solution.py
+++ b/solution.py
@@ -131,7 +131,7 @@
             pltpu.VMEM((3, TOK + half, WIN_LANES), jnp.bfloat16),
             pltpu.VMEM((TOK, WIN_LANES), jnp.bfloat16),
         ],
-        compiler_params=pltpu.CompilerParams(vmem_limit_bytes=24 * 2**20),
+        compiler_params=pltpu.CompilerParams(vmem_limit_bytes=14 * 2**20),
         name="window_attention",
     )(offset, own, below)
 
@@ -157,7 +157,7 @@
         tile_kernel,
         out_shape=jax.ShapeDtypeStruct((TOK, SW), jnp.bfloat16),
         scratch_shapes=[pltpu.VMEM((TOK, SW), jnp.bfloat16)],
-        compiler_params=pltpu.CompilerParams(vmem_limit_bytes=16 * 2**20),
+        compiler_params=pltpu.CompilerParams(vmem_limit_bytes=12 * 2**20),
         name="tile_attention",
     )(own)
 
@@ -180,10 +180,19 @@
 
 def project_kernel(
     place_ref, own_ref, left_ref, right_ref, far_a_ref, far_b_ref, shard_ref, mine_ref, other_ref,
-    out_ref, weights, sems,
+    out_ref, tokens, weights, sems,
 ):
     core, y, zh = place_ref[0], place_ref[1], place_ref[2]
     copies = []
+    row = 0
+    for src in (own_ref, left_ref, right_ref, far_a_ref, far_b_ref):
+        copies.append(
+            pltpu.make_async_copy(
+                src, tokens.at[pl.ds(row, src.shape[0]), :], sems.at[len(copies)]
+            )
+        )
+        copies[-1].start()
+        row += src.shape[0]
 
     def fetch(src, piece, part):
         rows = pl.ds(pl.multiple_of(part * SHARD, SHARD), SHARD)
@@ -203,9 +212,6 @@
                     lax.rem(zh + dz + 4, 4),
                 )
     weights[:, CHUNK:, :] = jnp.zeros((PIECES, CHUNK_PAD - CHUNK, PIECE), jnp.bfloat16)
-    tokens = jnp.concatenate(
-        [own_ref[...], left_ref[...], right_ref[...], far_a_ref[...], far_b_ref[...]], axis=0
-    )
     for copy in copies:
         copy.wait()
     for n in range(CHUNK_PAD // N_BLOCK):
@@ -213,7 +219,7 @@
         part = [weights[j, rows, :] for j in range(PIECES - 1)]
         part.append(weights[PIECES - 1, rows, 2 * LANES :])
         result = lax.dot_general(
-            tokens,
+            tokens[...],
             jnp.concatenate(part, axis=1),
             (((1,), (1,)), ((), ())),
             preferred_element_type=jnp.float32,
@@ -225,43 +231,38 @@
 
 def project(place, tokens, shard, mine, other):
     vmem = pl.BlockSpec(memory_space=pltpu.VMEM)
-    hbm = pl.BlockSpec(memory_space=pl.ANY)
+    hbm = pl.BlockSpec(memory_space=pltpu.HBM)
+    anywhere = pl.BlockSpec(memory_space=pl.ANY)
     return pl.pallas_call(
         project_kernel,
-        in_specs=[pl.BlockSpec(memory_space=pltpu.SMEM)] + [vmem] * 5 + [hbm] * 3,
+        in_specs=[pl.BlockSpec(memory_space=pltpu.SMEM)] + [hbm] * 5 + [anywhere] * 3,
         out_specs=vmem,
         out_shape=jax.ShapeDtypeStruct((COLS, XS * ROWS, CHUNK_PAD), jnp.bfloat16),
         scratch_shapes=[
+            pltpu.VMEM((XS * TOK, HRW), jnp.bfloat16),
             pltpu.VMEM((PIECES, CHUNK_PAD, PIECE), jnp.bfloat16),
-            pltpu.SemaphoreType.DMA((PIECES + 24,)),
-        ],
-        compiler_params=pltpu.CompilerParams(vmem_limit_bytes=40 * 2**20),
+            pltpu.SemaphoreType.DMA((PIECES + 24 + 5,)),
+        ],
+        compiler_params=pltpu.CompilerParams(vmem_limit_bytes=20 * 2**20),
         name="project",
     )(place, *tokens, shard, mine, other)
 
 
-def s_project_kernel(
-    place_ref, tokens_ref, own_ref, left_ref, right_ref, far_a_ref, far_b_ref, out_ref, weights
-):
+def s_project_kernel(place_ref, tokens_ref, mine_ref, other_ref, out_ref, weights):
     core, y, zh, x = [place_ref[i] for i in range(4)]
-    blocks = [(j, zh) for j in range(PIECES)]
-    for c in (core, 1 - core):
+    for raw_ref, c in ((mine_ref, core), (other_ref, 1 - core)):
+        blocks = [(c * 4 + i, zh) for i in range(4)]
         for dy in NEAR_Y:
             for dz in NEAR_Z:
                 blocks.append((c * 4 + lax.rem(y + dy + 4, 4), lax.rem(zh + dz + 4, 4)))
-    for b, dx in enumerate(NEAR_Y):
-        xs = lax.rem(x + dx + 4, 4)
-        for i, (j, zs) in enumerate(blocks):
-            if b < 3:
-                block = (own_ref, left_ref, right_ref)[b][i]
-            elif i < 16:
-                block = far_a_ref[i]
-            else:
-                block = far_b_ref[i - 16]
-            row = (xs * ZS + zs) * S_SHARD
-            for half in range(2):
-                rows = pl.ds(pl.multiple_of(row + half * S_ROWS, S_ROWS), S_ROWS)
-                weights[j, rows, :] = block[:, half * LANES : (half + 1) * LANES]
+        for b, dx in enumerate(NEAR_Y):
+            xs = lax.rem(x + dx + 4, 4)
+            for i, (j, zs) in enumerate(blocks):
+                block = raw_ref[b * len(blocks) + i]
+                row = (xs * ZS + zs) * S_SHARD
+                for half in range(2):
+                    rows = pl.ds(pl.multiple_of(row + half * S_ROWS, S_ROWS), S_ROWS)
+                    weights[j, rows, :] = block[:, half * LANES : (half + 1) * LANES]
     for n in range(SW // N_BLOCK):
         part = jnp.concatenate([weights[2 * n], weights[2 * n + 1]], axis=1)
         out_ref[:, n * N_BLOCK : (n + 1) * N_BLOCK] = jnp.dot(
@@ -269,16 +270,16 @@
         ).astype(jnp.bfloat16)
 
 
-def s_project(place, tokens, raw):
+def s_project(place, tokens, mine, other):
     return pl.pallas_call(
         s_project_kernel,
         in_specs=[pl.BlockSpec(memory_space=pltpu.SMEM)]
-        + [pl.BlockSpec(memory_space=pltpu.VMEM)] * 6,
+        + [pl.BlockSpec(memory_space=pltpu.VMEM)] * 3,
         out_shape=jax.ShapeDtypeStruct((TOK, SW), jnp.bfloat16),
         scratch_shapes=[pltpu.VMEM((PIECES, SW, LANES), jnp.bfloat16)],
-        compiler_params=pltpu.CompilerParams(vmem_limit_bytes=16 * 2**20),
+        compiler_params=pltpu.CompilerParams(vmem_limit_bytes=12 * 2**20),
         name="s_project",
-    )(place, tokens, *raw)
+    )(place, tokens, mine, other)
 
 
 HR_GROUPS = CHUNK_PAD // LANES
@@ -348,7 +349,7 @@
         merge_kernel,
         out_shape=jax.ShapeDtypeStruct((TOK, F), jnp.bfloat16),
         scratch_shapes=[pltpu.VMEM((GROUPS, TOK, LANES), jnp.float32)],
-        compiler_params=pltpu.CompilerParams(vmem_limit_bytes=40 * 2**20),
+        compiler_params=pltpu.CompilerParams(vmem_limit_bytes=16 * 2**20),
         name="merge",
     )(
         hr, s_out, valid, padded(embed), embed[:, HRW:], padded(gain), gain[:, HRW:]
@@ -394,10 +395,12 @@
     near = neighbours(piece, "zh")
 
     tile_out = tile_attention(s_qkv.reshape(3, TOK, SW))
-    below = after(below, tile_out, near)
+    s_tokens = lax.all_to_all(
+        tile_out.reshape(COLS, ROWS, SW), DATE, split_axis=0, concat_axis=0, tiled=True
+    )
     window_out, passed = window_attention(shifts, own, below)
-    above = ring(passed, SPACE, 1)
-    near = after(near, window_out)
+    above = ring(after(passed, near), SPACE, 1)
+    near = after(near, window_out, s_tokens)
     foreign = jnp.concatenate(near + opposite(near, "zh"), axis=0)
 
     window_out = window_out.reshape(COLS, ROWS, HRW)
@@ -410,18 +413,14 @@
     mine = after(mine, far)
     other = ring(mine, "core", 1)
 
-    s_tokens = lax.all_to_all(
-        tile_out.reshape(COLS, ROWS, SW), DATE, split_axis=0, concat_axis=0, tiled=True
-    )
     hr_out = project(place, (window_out,) + beside + far, shard, mine, other)
+    raw = after(mine, hr_out).reshape(-1, PIECE_ROWS, PIECE)[:, SHARD:, : 2 * LANES]
     hr_out = lax.all_to_all(hr_out, DATE, split_axis=0, concat_axis=0, tiled=True)
 
-    raw = [
-        part.reshape(-1, PIECE_ROWS, PIECE)[:, SHARD:, : 2 * LANES] for part in (mine, other)
-    ]
-    raw = jnp.concatenate([s_shard] + raw, axis=0)
+    raw = jnp.concatenate([lax.dynamic_slice_in_dim(s_shard, core * 4, 4), raw], axis=0)
     near = neighbours(raw, "x")
-    s_out = s_project(place, s_tokens.reshape(TOK, SW), (raw,) + near + opposite(near, "x"))
+    raw = jnp.concatenate((raw,) + near + opposite(near, "x"), axis=0)
+    s_out = s_project(place, s_tokens.reshape(TOK, SW), raw, ring(raw, "core", 1))
 
     out = merge(
         hr_out,

time: 192 us -> 203 us (1.057)
  the two profiles are of different devices: /device:TPU:41 before, /device:TPU:32 now
where the time goes in v3:
time: 203 us; the launch traced here: 202 us
  starting transfers between devices  98.7 us (49%)
  waiting for transfers between devices  51.4 us (25%)
  local copies, waits for them, and re-layouts  29.3 us (14%)
  Pallas kernels  20 us (10%)
    ppermute x20, starting transfers between devices, ring(): return lax.ppermute(x, axis, [(i, (i + by) % size) for i in range(size)])  70.6 us
    ppermute x20, waiting for transfers between devices, ring(): return lax.ppermute(x, axis, [(i, (i + by) % size) for i in range(size)])  38.6 us
    all_to_all x1, starting transfers between devices, per_device(): lax.all_to_all(tile_out.reshape(COLS, ROWS, SW), DATE, split_axis=0, conc...  17.2 us
    unnamed x53, local copies, waits for them, and re-layouts  15.7 us
    all_to_all x1, waiting for transfers between devices, per_device(): lax.all_to_all(hr_out, DATE, split_axis=0, concat_axis=0, tiled=True)  12.9 us
    all_to_all x1, starting transfers between devices, per_device(): lax.all_to_all(hr_out, DATE, split_axis=0, concat_axis=0, tiled=True)  11 us
    pallas_call x1, Pallas kernels, project(): pl.pallas_call(project_kernel, in_specs=[pl.BlockSpec(memory_space=pltpu....  9.04 us
    pallas_call x1, Pallas kernels, window_attention(): pl.pallas_call(window_kernel, grid=(WIN_BLOCKS,), in_specs=[pl.BlockSpec(...  4.2 us
  transfers between devices with their start and end apart: 22, of which 13 were waited for; matrix products, arithmetic and copies ran while one was open for 10% of the time, Pallas kernels for 4%

profile of v3, /device:TPU:32, one launch (start us, length us, event | category | flops | bytes accessed | tf_op | source)
XLA Modules:
  0.0 201.6 jit_solution(16608714401572098254)
XLA Ops:
  0.0 2.4 %slice.64 = bf16[3,64,2816]{2,1,0:T(8,128)(2,1)} slice(bf16[3,128,2816]{2,1,0:T(8,128)(2,1)} %bitcast.33), slice={[0:3], [0:64], [0:2816]} | slice | bytes 2162688 | tf_op jit(solution)/shard_map/slice | solution.py:382
  2.4 2.0 %collective-permute-start = (bf16[3,64,2816]{2,1,0:T(8,128)(2,1)}, bf16[3,64,2816]{2,1,0:T(8,128)(2,1)S(1)}, u32[]{:S(2)}, u32[]{:S(2)}) collective-permute-start(bf16[3,64,2816]{2,1,0:T(8,128)(2,1)} %slice.64), channel_id=1, source_target_pairs={{0,496},{16,0},{32,16},{48,32},{64,48},{80,64},{96,80},{112,96},{1... | collective-permute-start | bytes 3244040 | tf_op jit(solution)/shard_map/ppermute | solution.py:361
  4.5 1.6 tile_attention.1
  6.0 17.2 %all-to-all-start = ((bf16[16,8,1024]{2,1,0:T(8,128)(2,1)}), bf16[16,8,1024]{2,1,0:T(8,128)(2,1)S(1)}, u32[]{:S(2)}, u32[]{:S(2)}) async-start(bf16[16,8,1024]{2,1,0:T(8,128)(2,1)} %bitcast.12), calls=%async_computation | async-start | bytes 524288 | tf_op jit(solution)/shard_map/all_to_all | solution.py:398
  23.3 0.9 copy.15
  24.2 0.8 copy.19
  25.0 1.7 reshape.54
  26.6 0.7 dynamic-slice_bitcast_fusion.1
  27.4 1.0 dynamic-slice_bitcast_fusion
  28.4 7.7 %collective-permute-start.1 = (bf16[208,384]{1,0:T(8,128)(2,1)S(1)}, bf16[208,384]{1,0:T(8,128)(2,1)S(1)}, u32[]{:S(2)}, u32[]{:S(2)}) collective-permute-start(bf16[208,384]{1,0:T(8,128)(2,1)S(1)} %fusion.1), channel_id=1, source_target_pairs={{0,1},{1,2},{2,3},{3,0},{4,5},{5,6},{6,7},{7,4},{8,9},{9,10},{10,1... | collective-permute-start | bytes 479240 | tf_op jit(solution)/shard_map/ppermute | solution.py:361
  36.1 2.0 %collective-permute-start.2 = (bf16[208,384]{1,0:T(8,128)(2,1)S(1)}, bf16[208,384]{1,0:T(8,128)(2,1)S(1)}, u32[]{:S(2)}, u32[]{:S(2)}) collective-permute-start(bf16[208,384]{1,0:T(8,128)(2,1)S(1)} %fusion.1), channel_id=1, source_target_pairs={{0,3},{1,0},{2,1},{3,2},{4,7},{5,4},{6,5},{7,6},{8,11},{9,8},{10,9... | collective-permute-start | bytes 479240 | tf_op jit(solution)/shard_map/ppermute | solution.py:361
  38.8 4.2 %window_attention.1 = (bf16[128,2816]{1,0:T(8,128)(2,1)S(1)}, bf16[64,2816]{1,0:T(8,128)(2,1)}) custom-call(s32[1]{0:T(128)S(6)} %copy.35.offset_ref, bf16[3,128,2816]{2,1,0:T(8,128)(2,1)S(1)} %bitcast.34, bf16[3,64,2816]{2,1,0:T(8,128)(2,1)S(1)} %collective-permute-done.below_ref), custom_call_target="tpu_custom_call" | custom-call | tf_op jit(solution)/shard_map/window_attention/pallas_call | solution.py:114
  43.0 0.9 copy-done.7
  43.9 8.2 %collective-permute-done.1 = bf16[208,384]{1,0:T(8,128)(2,1)S(1)} collective-permute-done((bf16[208,384]{1,0:T(8,128)(2,1)S(1)}, bf16[208,384]{1,0:T(8,128)(2,1)S(1)}, u32[]{:S(2)}, u32[]{:S(2)}) %collective-permute-start.1) | collective-permute-done | bytes 159776 | tf_op jit(solution)/shard_map/ppermute | solution.py:361
  52.1 4.2 %collective-permute-done.2 = bf16[208,384]{1,0:T(8,128)(2,1)S(1)} collective-permute-done((bf16[208,384]{1,0:T(8,128)(2,1)S(1)}, bf16[208,384]{1,0:T(8,128)(2,1)S(1)}, u32[]{:S(2)}, u32[]{:S(2)}) %collective-permute-start.2) | collective-permute-done | bytes 159776 | tf_op jit(solution)/shard_map/ppermute | solution.py:361
  56.3 0.7 copy-done.14
  56.9 1.9 collective-permute-start.3
  58.9 1.6 slice.53
  60.4 6.8 %collective-permute-start.8 = (bf16[104,384]{1,0:T(8,128)(2,1)}, bf16[104,384]{1,0:T(8,128)(2,1)}, u32[]{:S(2)}, u32[]{:S(2)}) collective-permute-start(bf16[104,384]{1,0:T(8,128)(2,1)} %slice.53), channel_id=1, source_target_pairs={{0,1},{1,2},{2,3},{3,0},{4,5},{5,6},{6,7},{7,4},{8,9},{9,10},{10,1... | collective-permute-start | bytes 239624 | tf_op jit(solution)/shard_map/ppermute | solution.py:361
  67.3 1.5 slice.54
  68.8 2.9 %collective-permute-start.9 = (bf16[104,384]{1,0:T(8,128)(2,1)}, bf16[104,384]{1,0:T(8,128)(2,1)}, u32[]{:S(2)}, u32[]{:S(2)}) collective-permute-start(bf16[104,384]{1,0:T(8,128)(2,1)} %slice.54), channel_id=1, source_target_pairs={{0,3},{1,0},{2,1},{3,2},{4,7},{5,4},{6,5},{7,6},{8,11},{9,8},{10,9... | collective-permute-start | bytes 239624 | tf_op jit(solution)/shard_map/ppermute | solution.py:361
  71.7 1.6 constant_dynamic-update-slice_fusion.3
  73.3 1.1 reshape.55
  75.1 3.4 %collective-permute-start.4 = (bf16[128,2816]{1,0:T(8,128)(2,1)S(1)}, bf16[128,2816]{1,0:T(8,128)(2,1)S(1)}, u32[]{:S(2)}, u32[]{:S(2)}) collective-permute-start(bf16[128,2816]{1,0:T(8,128)(2,1)S(1)} %maximum_bitcast_fusion.own_ref), channel_id=1, source_target_pairs={{0,4},{4,8},{8,12},{12,0},{1,5},{5,9},{9,13},{13,1},{2,6},{6,10},{... | collective-permute-start | bytes 2162696 | tf_op jit(solution)/shard_map/ppermute | solution.py:361
  78.6 3.7 %collective-permute-start.5 = (bf16[128,2816]{1,0:T(8,128)(2,1)S(1)}, bf16[128,2816]{1,0:T(8,128)(2,1)S(1)}, u32[]{:S(2)}, u32[]{:S(2)}) collective-permute-start(bf16[128,2816]{1,0:T(8,128)(2,1)S(1)} %maximum_bitcast_fusion.own_ref), channel_id=1, source_target_pairs={{0,12},{4,0},{8,4},{12,8},{1,13},{5,1},{9,5},{13,9},{2,14},{6,2},{... | collective-permute-start | bytes 2162696 | tf_op jit(solution)/shard_map/ppermute | solution.py:361
  82.2 1.0 constant_dynamic-update-slice_fusion.2
  83.2 0.9 constant_dynamic-update-slice_fusion.1
  84.1 0.9 constant_dynamic-update-slice_fusion
  85.0 3.5 %collective-permute-start.10 = (bf16[624,384]{1,0:T(8,128)(2,1)S(1)}, bf16[624,384]{1,0:T(8,128)(2,1)S(1)}, u32[]{:S(2)}, u32[]{:S(2)}) collective-permute-start(bf16[624,384]{1,0:T(8,128)(2,1)S(1)} %get-tuple-element.33), channel_id=1, source_target_pairs={{0,128},{128,256},{256,384},{384,0},{1,129},{129,257},{257,385},{3... | collective-permute-start | bytes 1437704 | tf_op jit(solution)/shard_map/ppermute | solution.py:361
  88.6 3.6 %collective-permute-start.11 = (bf16[624,384]{1,0:T(8,128)(2,1)S(1)}, bf16[624,384]{1,0:T(8,128)(2,1)S(1)}, u32[]{:S(2)}, u32[]{:S(2)}) collective-permute-start(bf16[624,384]{1,0:T(8,128)(2,1)S(1)} %get-tuple-element.33), channel_id=1, source_target_pairs={{0,384},{128,0},{256,128},{384,256},{1,385},{129,1},{257,129},{385... | collective-permute-start | bytes 1437704 | tf_op jit(solution)/shard_map/ppermute | solution.py:361
  92.1 8.7 %collective-permute-done.10 = bf16[624,384]{1,0:T(8,128)(2,1)S(1)} collective-permute-done((bf16[624,384]{1,0:T(8,128)(2,1)S(1)}, bf16[624,384]{1,0:T(8,128)(2,1)S(1)}, u32[]{:S(2)}, u32[]{:S(2)}) %collective-permute-start.10) | collective-permute-done | bytes 479264 | tf_op jit(solution)/shard_map/ppermute | solution.py:361
  100.9 1.9 collective-permute-done.11
  102.9 3.5 %collective-permute-start.12 = (bf16[312,384]{1,0:T(8,128)(2,1)S(1)}, bf16[312,384]{1,0:T(8,128)(2,1)S(1)}, u32[]{:S(2)}, u32[]{:S(2)}) collective-permute-start(bf16[312,384]{1,0:T(8,128)(2,1)S(1)} %slice.55), channel_id=1, source_target_pairs={{0,128},{128,256},{256,384},{384,0},{1,129},{129,257},{257,385},{3... | collective-permute-start | bytes 718856 | tf_op jit(solution)/shard_map/ppermute | solution.py:361
  106.4 3.6 %collective-permute-start.13 = (bf16[312,384]{1,0:T(8,128)(2,1)S(1)}, bf16[312,384]{1,0:T(8,128)(2,1)S(1)}, u32[]{:S(2)}, u32[]{:S(2)}) collective-permute-start(bf16[312,384]{1,0:T(8,128)(2,1)S(1)} %slice.56), channel_id=1, source_target_pairs={{0,384},{128,0},{256,128},{384,256},{1,385},{129,1},{257,129},{385... | collective-permute-start | bytes 718856 | tf_op jit(solution)/shard_map/ppermute | solution.py:361
  110.0 2.4 %collective-permute-start.6 = (bf16[64,2816]{1,0:T(8,128)(2,1)S(1)}, bf16[64,2816]{1,0:T(8,128)(2,1)S(1)}, u32[]{:S(2)}, u32[]{:S(2)}) collective-permute-start(bf16[64,2816]{1,0:T(8,128)(2,1)S(1)} %slice.67), channel_id=1, source_target_pairs={{0,4},{4,8},{8,12},{12,0},{1,5},{5,9},{9,13},{13,1},{2,6},{6,10},{... | collective-permute-start | bytes 1081352 | tf_op jit(solution)/shard_map/ppermute | solution.py:361
  112.5 4.6 %collective-permute-start.7 = (bf16[64,2816]{1,0:T(8,128)(2,1)S(1)}, bf16[64,2816]{1,0:T(8,128)(2,1)S(1)}, u32[]{:S(2)}, u32[]{:S(2)}) collective-permute-start(bf16[64,2816]{1,0:T(8,128)(2,1)S(1)} %slice.68), channel_id=1, source_target_pairs={{0,12},{4,0},{8,4},{12,8},{1,13},{5,1},{9,5},{13,9},{2,14},{6,2},{... | collective-permute-start | bytes 1081352 | tf_op jit(solution)/shard_map/ppermute | solution.py:361
  117.4 4.1 %collective-permute-done.6.far_a_ref = bf16[64,2816]{1,0:T(8,128)(2,1)S(1)} collective-permute-done((bf16[64,2816]{1,0:T(8,128)(2,1)S(1)}, bf16[64,2816]{1,0:T(8,128)(2,1)S(1)}, u32[]{:S(2)}, u32[]{:S(2)}) %collective-permute-start.6) | collective-permute-done | bytes 360480 | tf_op jit(solution)/shard_map/ppermute | solution.py:361
  121.5 0.7 copy-done.9
  122.2 0.5 collective-permute-done.7.far_b_ref
  122.7 0.7 copy-done.11
  123.5 1.9 collective-permute-start.14
  125.5 3.9 %collective-permute-done.14.other_ref = bf16[2496,384]{1,0:T(8,128)(2,1)} collective-permute-done((bf16[2496,384]{1,0:T(8,128)(2,1)S(1)}, bf16[2496,384]{1,0:T(8,128)(2,1)}, u32[]{:S(2)}, u32[]{:S(2)}) %collective-permute-start.14) | collective-permute-done | bytes 1916960 | tf_op jit(solution)/shard_map/ppermute | solution.py:361
  129.4 1.1 copy-done.2
  130.5 1.2 copy-done.3
  131.7 1.0 copy-done.10
  132.7 1.0 copy-done.12
  133.7 9.0 %project.1 = bf16[16,32,768]{2,1,0:T(8,128)(2,1)} custom-call(s32[4]{0:T(128)S(1)} %pad_add_fusion.place_ref, bf16[128,2816]{1,0:T(8,128)(2,1)S(1)} %maximum_bitcast_fusion.own_ref, bf16[128,2816]{1,0:T(8,128)(2,1)S(1)} %collective-permute-done.4.left_ref, bf16[128,2816]{1,0:T(8,128)(2,1)S(1)} %copy-done.2, bf16[64,2816]{1,0:T(8,128)(2,1)S(1)} %copy-done.10, ...), custom_call_target="tpu_custom_call" | custom-call | tf_op jit(solution)/shard_map/project/pallas_call | solution.py:236
  142.7 11.0 %all-to-all-start.1 = ((bf16[16,32,768]{2,1,0:T(8,128)(2,1)}), bf16[16,32,768]{2,1,0:T(8,128)(2,1)S(1)}, u32[]{:S(2)}, u32[]{:S(2)}) async-start(bf16[16,32,768]{2,1,0:T(8,128)(2,1)} %project.1), calls=%async_computation.1 | async-start | bytes 1572864 | tf_op jit(solution)/shard_map/all_to_all | solution.py:418
  153.7 1.6 constant_dynamic-update-slice_fusion.17
  155.3 0.7 fusion.2
  156.1 4.0 %collective-permute-start.15 = (bf16[16,32,256]{2,1,0:T(8,128)(2,1)S(1)}, bf16[16,32,256]{2,1,0:T(8,128)(2,1)S(1)}, u32[]{:S(2)}, u32[]{:S(2)}) collective-permute-start(bf16[16,32,256]{2,1,0:T(8,128)(2,1)S(1)} %pad_maximum_fusion), channel_id=1, source_target_pairs={{0,4},{4,8},{8,12},{12,0},{1,5},{5,9},{9,13},{13,1},{2,6},{6,10},{... | collective-permute-start | bytes 786440 | tf_op jit(solution)/shard_map/ppermute | solution.py:361
  160.0 3.2 %collective-permute-start.16 = (bf16[16,32,256]{2,1,0:T(8,128)(2,1)S(1)}, bf16[16,32,256]{2,1,0:T(8,128)(2,1)S(1)}, u32[]{:S(2)}, u32[]{:S(2)}) collective-permute-start(bf16[16,32,256]{2,1,0:T(8,128)(2,1)S(1)} %pad_maximum_fusion), channel_id=1, source_target_pairs={{0,12},{4,0},{8,4},{12,8},{1,13},{5,1},{9,5},{13,9},{2,14},{6,2},{... | collective-permute-start | bytes 786440 | tf_op jit(solution)/shard_map/ppermute | solution.py:361
  163.3 4.2 %collective-permute-done.15 = bf16[16,32,256]{2,1,0:T(8,128)(2,1)S(1)} collective-permute-done((bf16[16,32,256]{2,1,0:T(8,128)(2,1)S(1)}, bf16[16,32,256]{2,1,0:T(8,128)(2,1)S(1)}, u32[]{:S(2)}, u32[]{:S(2)}) %collective-permute-start.15) | collective-permute-done | bytes 262176 | tf_op jit(solution)/shard_map/ppermute | solution.py:361
  167.5 3.0 %collective-permute-start.17 = (bf16[8,32,256]{2,1,0:T(8,128)(2,1)S(1)}, bf16[8,32,256]{2,1,0:T(8,128)(2,1)S(1)}, u32[]{:S(2)}, u32[]{:S(2)}) collective-permute-start(bf16[8,32,256]{2,1,0:T(8,128)(2,1)S(1)} %slice.70), channel_id=1, source_target_pairs={{0,4},{4,8},{8,12},{12,0},{1,5},{5,9},{9,13},{13,1},{2,6},{6,10},{... | collective-permute-start | bytes 393224 | tf_op jit(solution)/shard_map/ppermute | solution.py:361
  170.7 4.7 %collective-permute-start.18 = (bf16[8,32,256]{2,1,0:T(8,128)(2,1)S(1)}, bf16[8,32,256]{2,1,0:T(8,128)(2,1)S(1)}, u32[]{:S(2)}, u32[]{:S(2)}) collective-permute-start(bf16[8,32,256]{2,1,0:T(8,128)(2,1)S(1)} %slice.71), channel_id=1, source_target_pairs={{0,12},{4,0},{8,4},{12,8},{1,13},{5,1},{9,5},{13,9},{2,14},{6,2},{... | collective-permute-start | bytes 393224 | tf_op jit(solution)/shard_map/ppermute | solution.py:361
  175.4 0.7 constant_dynamic-update-slice_fusion.15
  176.2 0.7 constant_dynamic-update-slice_fusion.14
  177.3 0.7 constant_dynamic-update-slice_fusion.13
  178.1 0.7 constant_dynamic-update-slice_fusion.12.mine_ref
  178.8 2.1 %collective-permute-start.19 = (bf16[64,32,256]{2,1,0:T(8,128)(2,1)}, bf16[64,32,256]{2,1,0:T(8,128)(2,1)S(1)}, u32[]{:S(2)}, u32[]{:S(2)}) collective-permute-start(bf16[64,32,256]{2,1,0:T(8,128)(2,1)} %constant_dynamic-update-slice_fusion.12.mine_ref), channel_id=1, source_target_pairs={{0,16},{16,0},{1,17},{17,1},{2,18},{18,2},{3,19},{19,3},{4,20},{20... | collective-permute-start | bytes 3145736 | tf_op jit(solution)/shard_map/ppermute | solution.py:361
  181.5 2.0 %collective-permute-done.19.other_ref = bf16[64,32,256]{2,1,0:T(8,128)(2,1)S(1)} collective-permute-done((bf16[64,32,256]{2,1,0:T(8,128)(2,1)}, bf16[64,32,256]{2,1,0:T(8,128)(2,1)S(1)}, u32[]{:S(2)}, u32[]{:S(2)}) %collective-permute-start.19) | collective-permute-done | bytes 1048608 | tf_op jit(solution)/shard_map/ppermute | solution.py:361
  183.5 2.0 s_project.1.s_ref
  185.5 12.9 %all-to-all-done.1.hr_ref = bf16[16,32,768]{2,1,0:T(8,128)(2,1)S(1)} async-done(((bf16[16,32,768]{2,1,0:T(8,128)(2,1)}), bf16[16,32,768]{2,1,0:T(8,128)(2,1)S(1)}, u32[]{:S(2)}, u32[]{:S(2)}) %all-to-all-start.1) | async-done | bytes 786464 | tf_op jit(solution)/shard_map/all_to_all | solution.py:418
  198.4 3.2 %merge.1 = bf16[128,3840]{1,0:T(8,128)(2,1)} custom-call(bf16[16,32,768]{2,1,0:T(8,128)(2,1)S(1)} %all-to-all-done.1.hr_ref, bf16[128,1024]{1,0:T(8,128)(2,1)S(1)} %s_project.1.s_ref, s32[1,128]{1,0:T(1,128)S(1)} %reshape.61.valid_ref, bf16[16,3072]{1,0:T(8,128)(2,1)S(1)} %bitcast.40, bf16[16,1024]{1,0:T(8,128)(2,1)S(1)} %slice.61.s_embed_ref, ...), custom_call_target="tpu_custom_call" | custom-call | tf_op jit(solution)/shard_map/merge/pallas_call | solution.py:348
  (71 shorter events, 2.5 us)
Async XLA Ops:
  0.0 4.4 %copy-start.6 = (bf16[3,1,8,16,1024]{4,3,2,1,0:T(8,128)(2,1)S(1)}, bf16[3,1,8,16,1024]{4,3,2,1,0:T(8,128)(2,1)}, u32[]{:S(2)}) copy-start(bf16[3,1,8,16,1024]{4,3,2,1,0:T(8,128)(2,1)} %param.9) | copy-start | bytes 2359300
  2.4 36.4 %copy-start = (bf16[3,1,8,16,2816]{4,3,2,1,0:T(8,128)(2,1)S(1)}, bf16[3,1,8,16,2816]{4,3,2,1,0:T(8,128)(2,1)}, u32[]{:S(2)}) copy-start(bf16[3,1,8,16,2816]{4,3,2,1,0:T(8,128)(2,1)} %param.8) | copy-start | bytes 6488068
  2.4 36.4 %collective-permute-start = (bf16[3,64,2816]{2,1,0:T(8,128)(2,1)}, bf16[3,64,2816]{2,1,0:T(8,128)(2,1)S(1)}, u32[]{:S(2)}, u32[]{:S(2)}) collective-permute-start(bf16[3,64,2816]{2,1,0:T(8,128)(2,1)} %slice.64), channel_id=1, source_target_pairs={{0,496},{16,0},{32,16},{48,32},{64,48},{80,64},{96,80},{112,96},{1... | collective-permute-start | bytes 3244040 | tf_op jit(solution)/shard_map/ppermute | solution.py:361
  6.0 52.8 %all-to-all-start = ((bf16[16,8,1024]{2,1,0:T(8,128)(2,1)}), bf16[16,8,1024]{2,1,0:T(8,128)(2,1)S(1)}, u32[]{:S(2)}, u32[]{:S(2)}) async-start(bf16[16,8,1024]{2,1,0:T(8,128)(2,1)} %bitcast.12), calls=%async_computation | async-start | bytes 524288 | tf_op jit(solution)/shard_map/all_to_all | solution.py:398
  28.4 23.7 %collective-permute-start.1 = (bf16[208,384]{1,0:T(8,128)(2,1)S(1)}, bf16[208,384]{1,0:T(8,128)(2,1)S(1)}, u32[]{:S(2)}, u32[]{:S(2)}) collective-permute-start(bf16[208,384]{1,0:T(8,128)(2,1)S(1)} %fusion.1), channel_id=1, source_target_pairs={{0,1},{1,2},{2,3},{3,0},{4,5},{5,6},{6,7},{7,4},{8,9},{9,10},{10,1... | collective-permute-start | bytes 479240 | tf_op jit(solution)/shard_map/ppermute | solution.py:361
  36.1 20.1 %collective-permute-start.2 = (bf16[208,384]{1,0:T(8,128)(2,1)S(1)}, bf16[208,384]{1,0:T(8,128)(2,1)S(1)}, u32[]{:S(2)}, u32[]{:S(2)}) collective-permute-start(bf16[208,384]{1,0:T(8,128)(2,1)S(1)} %fusion.1), channel_id=1, source_target_pairs={{0,3},{1,0},{2,1},{3,2},{4,7},{5,4},{6,5},{7,6},{8,11},{9,8},{10,9... | collective-permute-start | bytes 479240 | tf_op jit(solution)/shard_map/ppermute | solution.py:361
  43.0 0.9 copy-start.7
  52.1 4.2 %copy-start.15 = (bf16[208,384]{1,0:T(8,128)(2,1)}, bf16[208,384]{1,0:T(8,128)(2,1)S(1)}, u32[]{:S(2)}) copy-start(bf16[208,384]{1,0:T(8,128)(2,1)S(1)} %collective-permute-done.1) | copy-start | bytes 479236
  52.1 22.3 %copy-start.8 = (bf16[128,2816]{1,0:T(8,128)(2,1)S(1)}, bf16[128,2816]{1,0:T(8,128)(2,1)}, u32[]{:S(2)}) copy-start(bf16[128,2816]{1,0:T(8,128)(2,1)} %copy-done.7) | copy-start | bytes 2162692
  56.3 0.7 copy-start.14
  56.9 16.4 %collective-permute-start.3 = (bf16[64,2816]{1,0:T(8,128)(2,1)}, bf16[64,2816]{1,0:T(8,128)(2,1)}, u32[]{:S(2)}, u32[]{:S(2)}) collective-permute-start(bf16[64,2816]{1,0:T(8,128)(2,1)} %get-tuple-element.16), channel_id=1, source_target_pairs={{0,16},{16,32},{32,48},{48,64},{64,80},{80,96},{96,112},{112,128},... | collective-permute-start | bytes 1081352 | tf_op jit(solution)/shard_map/ppermute | solution.py:361
  58.8 15.9 %copy-start.4 = (bf16[16,8,1024]{2,1,0:T(8,128)(2,1)}, bf16[16,8,1024]{2,1,0:T(8,128)(2,1)S(1)}, u32[]{:S(2)}) copy-start(bf16[16,8,1024]{2,1,0:T(8,128)(2,1)S(1)} %all-to-all-done) | copy-start | bytes 786436
  60.4 22.8 %collective-permute-start.8 = (bf16[104,384]{1,0:T(8,128)(2,1)}, bf16[104,384]{1,0:T(8,128)(2,1)}, u32[]{:S(2)}, u32[]{:S(2)}) collective-permute-start(bf16[104,384]{1,0:T(8,128)(2,1)} %slice.53), channel_id=1, source_target_pairs={{0,1},{1,2},{2,3},{3,0},{4,5},{5,6},{6,7},{7,4},{8,9},{9,10},{10,1... | collective-permute-start | bytes 239624 | tf_op jit(solution)/shard_map/ppermute | solution.py:361
  68.8 15.3 %collective-permute-start.9 = (bf16[104,384]{1,0:T(8,128)(2,1)}, bf16[104,384]{1,0:T(8,128)(2,1)}, u32[]{:S(2)}, u32[]{:S(2)}) collective-permute-start(bf16[104,384]{1,0:T(8,128)(2,1)} %slice.54), channel_id=1, source_target_pairs={{0,3},{1,0},{2,1},{3,2},{4,7},{5,4},{6,5},{7,6},{8,11},{9,8},{10,9... | collective-permute-start | bytes 239624 | tf_op jit(solution)/shard_map/ppermute | solution.py:361
  74.4 7.8 %copy-start.16 = (bf16[624,384]{1,0:T(8,128)(2,1)S(1)}, bf16[624,384]{1,0:T(8,128)(2,1)}, u32[]{:S(2)}) copy-start(bf16[624,384]{1,0:T(8,128)(2,1)} %get-tuple-element.31) | copy-start | bytes 1437700
  75.1 27.7 %collective-permute-start.4 = (bf16[128,2816]{1,0:T(8,128)(2,1)S(1)}, bf16[128,2816]{1,0:T(8,128)(2,1)S(1)}, u32[]{:S(2)}, u32[]{:S(2)}) collective-permute-start(bf16[128,2816]{1,0:T(8,128)(2,1)S(1)} %maximum_bitcast_fusion.own_ref), channel_id=1, source_target_pairs={{0,4},{4,8},{8,12},{12,0},{1,5},{5,9},{9,13},{13,1},{2,6},{6,10},{... | collective-permute-start | bytes 2162696 | tf_op jit(solution)/shard_map/ppermute | solution.py:361
  78.6 24.3 %collective-permute-start.5 = (bf16[128,2816]{1,0:T(8,128)(2,1)S(1)}, bf16[128,2816]{1,0:T(8,128)(2,1)S(1)}, u32[]{:S(2)}, u32[]{:S(2)}) collective-permute-start(bf16[128,2816]{1,0:T(8,128)(2,1)S(1)} %maximum_bitcast_fusion.own_ref), channel_id=1, source_target_pairs={{0,12},{4,0},{8,4},{12,8},{1,13},{5,1},{9,5},{13,9},{2,14},{6,2},{... | collective-permute-start | bytes 2162696 | tf_op jit(solution)/shard_map/ppermute | solution.py:361
  85.0 15.8 %collective-permute-start.10 = (bf16[624,384]{1,0:T(8,128)(2,1)S(1)}, bf16[624,384]{1,0:T(8,128)(2,1)S(1)}, u32[]{:S(2)}, u32[]{:S(2)}) collective-permute-start(bf16[624,384]{1,0:T(8,128)(2,1)S(1)} %get-tuple-element.33), channel_id=1, source_target_pairs={{0,128},{128,256},{256,384},{384,0},{1,129},{129,257},{257,385},{3... | collective-permute-start | bytes 1437704 | tf_op jit(solution)/shard_map/ppermute | solution.py:361
  88.6 14.3 %collective-permute-start.11 = (bf16[624,384]{1,0:T(8,128)(2,1)S(1)}, bf16[624,384]{1,0:T(8,128)(2,1)S(1)}, u32[]{:S(2)}, u32[]{:S(2)}) collective-permute-start(bf16[624,384]{1,0:T(8,128)(2,1)S(1)} %get-tuple-element.33), channel_id=1, source_target_pairs={{0,384},{128,0},{256,128},{384,256},{1,385},{129,1},{257,129},{385... | collective-permute-start | bytes 1437704 | tf_op jit(solution)/shard_map/ppermute | solution.py:361
  102.8 14.4 %copy-start.1 = (bf16[128,2816]{1,0:T(8,128)(2,1)}, bf16[128,2816]{1,0:T(8,128)(2,1)S(1)}, u32[]{:S(2)}) copy-start(bf16[128,2816]{1,0:T(8,128)(2,1)S(1)} %collective-permute-done.5.right_ref) | copy-start | bytes 2162692
  102.9 14.4 %collective-permute-start.12 = (bf16[312,384]{1,0:T(8,128)(2,1)S(1)}, bf16[312,384]{1,0:T(8,128)(2,1)S(1)}, u32[]{:S(2)}, u32[]{:S(2)}) collective-permute-start(bf16[312,384]{1,0:T(8,128)(2,1)S(1)} %slice.55), channel_id=1, source_target_pairs={{0,128},{128,256},{256,384},{384,0},{1,129},{129,257},{257,385},{3... | collective-permute-start | bytes 718856 | tf_op jit(solution)/shard_map/ppermute | solution.py:361
  106.4 11.0 %collective-permute-start.13 = (bf16[312,384]{1,0:T(8,128)(2,1)S(1)}, bf16[312,384]{1,0:T(8,128)(2,1)S(1)}, u32[]{:S(2)}, u32[]{:S(2)}) collective-permute-start(bf16[312,384]{1,0:T(8,128)(2,1)S(1)} %slice.56), channel_id=1, source_target_pairs={{0,384},{128,0},{256,128},{384,256},{1,385},{129,1},{257,129},{385... | collective-permute-start | bytes 718856 | tf_op jit(solution)/shard_map/ppermute | solution.py:361
  110.0 11.5 %collective-permute-start.6 = (bf16[64,2816]{1,0:T(8,128)(2,1)S(1)}, bf16[64,2816]{1,0:T(8,128)(2,1)S(1)}, u32[]{:S(2)}, u32[]{:S(2)}) collective-permute-start(bf16[64,2816]{1,0:T(8,128)(2,1)S(1)} %slice.67), channel_id=1, source_target_pairs={{0,4},{4,8},{8,12},{12,0},{1,5},{5,9},{9,13},{13,1},{2,6},{6,10},{... | collective-permute-start | bytes 1081352 | tf_op jit(solution)/shard_map/ppermute | solution.py:361
  112.5 10.3 %collective-permute-start.7 = (bf16[64,2816]{1,0:T(8,128)(2,1)S(1)}, bf16[64,2816]{1,0:T(8,128)(2,1)S(1)}, u32[]{:S(2)}, u32[]{:S(2)}) collective-permute-start(bf16[64,2816]{1,0:T(8,128)(2,1)S(1)} %slice.68), channel_id=1, source_target_pairs={{0,12},{4,0},{8,4},{12,8},{1,13},{5,1},{9,5},{13,9},{2,14},{6,2},{... | collective-permute-start | bytes 1081352 | tf_op jit(solution)/shard_map/ppermute | solution.py:361
  121.5 0.7 copy-start.9
  122.7 0.7 copy-start.11
  123.5 5.9 %collective-permute-start.14 = (bf16[2496,384]{1,0:T(8,128)(2,1)S(1)}, bf16[2496,384]{1,0:T(8,128)(2,1)}, u32[]{:S(2)}, u32[]{:S(2)}) collective-permute-start(bf16[2496,384]{1,0:T(8,128)(2,1)S(1)} %constant_dynamic-update-slice_fusion.4.mine_ref), channel_id=1, source_target_pairs={{0,16},{16,0},{1,17},{17,1},{2,18},{18,2},{3,19},{19,3},{4,20},{20... | collective-permute-start | bytes 5750792 | tf_op jit(solution)/shard_map/ppermute | solution.py:361
  129.4 1.1 copy-start.2
  130.5 1.2 copy-start.3
  131.7 1.0 copy-start.10
  132.7 1.0 copy-start.12
  142.7 55.6 %all-to-all-start.1 = ((bf16[16,32,768]{2,1,0:T(8,128)(2,1)}), bf16[16,32,768]{2,1,0:T(8,128)(2,1)S(1)}, u32[]{:S(2)}, u32[]{:S(2)}) async-start(bf16[16,32,768]{2,1,0:T(8,128)(2,1)} %project.1), calls=%async_computation.1 | async-start | bytes 1572864 | tf_op jit(solution)/shard_map/all_to_all | solution.py:418
  153.7 27.1 %copy-start.13 = (bf16[16,3840]{1,0:T(8,128)(2,1)S(1)}, bf16[16,3840]{1,0:T(8,128)(2,1)}, u32[]{:S(2)}) copy-start(bf16[16,3840]{1,0:T(8,128)(2,1)} %param.14) | copy-start | bytes 368644
  153.7 27.2 %copy-start.17 = (f32[3840]{0:T(1024)S(1)}, f32[3840]{0:T(1024)}, u32[]{:S(2)}) copy-start(f32[3840]{0:T(1024)} %param.15) | copy-start | bytes 46084
  153.7 27.3 %slice-start = ((bf16[16,3840]{1,0:T(8,128)(2,1)}), bf16[16,2816]{1,0:T(8,128)(2,1)S(1)}, s32[]{:S(2)}) async-start(bf16[16,3840]{1,0:T(8,128)(2,1)} %param.14), calls=%async_computation.2 | async-start | bytes 180224 | tf_op jit(solution)/shard_map/slice | solution.py:345
  156.0 25.3 %copy-start.18 = (s32[16,8,1]{0,2,1:T(1,128)S(1)}, s32[16,8,1]{0,2,1:T(1,128)}, u32[]{:S(2)}) copy-start(s32[16,8,1]{0,2,1:T(1,128)} %param.13) | copy-start | bytes 1540
  156.0 27.5 %copy-start.5 = (bf16[16,8,1024]{2,1,0:T(8,128)(2,1)S(1)}, bf16[16,8,1024]{2,1,0:T(8,128)(2,1)}, u32[]{:S(2)}) copy-start(bf16[16,8,1024]{2,1,0:T(8,128)(2,1)} %copy-done.4) | copy-start | bytes 786436
  156.1 11.4 %collective-permute-start.15 = (bf16[16,32,256]{2,1,0:T(8,128)(2,1)S(1)}, bf16[16,32,256]{2,1,0:T(8,128)(2,1)S(1)}, u32[]{:S(2)}, u32[]{:S(2)}) collective-permute-start(bf16[16,32,256]{2,1,0:T(8,128)(2,1)S(1)} %pad_maximum_fusion), channel_id=1, source_target_pairs={{0,4},{4,8},{8,12},{12,0},{1,5},{5,9},{9,13},{13,1},{2,6},{6,10},{... | collective-permute-start | bytes 786440 | tf_op jit(solution)/shard_map/ppermute | solution.py:361
  160.0 10.7 %collective-permute-start.16 = (bf16[16,32,256]{2,1,0:T(8,128)(2,1)S(1)}, bf16[16,32,256]{2,1,0:T(8,128)(2,1)S(1)}, u32[]{:S(2)}, u32[]{:S(2)}) collective-permute-start(bf16[16,32,256]{2,1,0:T(8,128)(2,1)S(1)} %pad_maximum_fusion), channel_id=1, source_target_pairs={{0,12},{4,0},{8,4},{12,8},{1,13},{5,1},{9,5},{13,9},{2,14},{6,2},{... | collective-permute-start | bytes 786440 | tf_op jit(solution)/shard_map/ppermute | solution.py:361
  167.5 9.9 %collective-permute-start.17 = (bf16[8,32,256]{2,1,0:T(8,128)(2,1)S(1)}, bf16[8,32,256]{2,1,0:T(8,128)(2,1)S(1)}, u32[]{:S(2)}, u32[]{:S(2)}) collective-permute-start(bf16[8,32,256]{2,1,0:T(8,128)(2,1)S(1)} %slice.70), channel_id=1, source_target_pairs={{0,4},{4,8},{8,12},{12,0},{1,5},{5,9},{9,13},{13,1},{2,6},{6,10},{... | collective-permute-start | bytes 393224 | tf_op jit(solution)/shard_map/ppermute | solution.py:361
  170.7 7.4 %collective-permute-start.18 = (bf16[8,32,256]{2,1,0:T(8,128)(2,1)S(1)}, bf16[8,32,256]{2,1,0:T(8,128)(2,1)S(1)}, u32[]{:S(2)}, u32[]{:S(2)}) collective-permute-start(bf16[8,32,256]{2,1,0:T(8,128)(2,1)S(1)} %slice.71), channel_id=1, source_target_pairs={{0,12},{4,0},{8,4},{12,8},{1,13},{5,1},{9,5},{13,9},{2,14},{6,2},{... | collective-permute-start | bytes 393224 | tf_op jit(solution)/shard_map/ppermute | solution.py:361
  178.8 4.8 %collective-permute-start.19 = (bf16[64,32,256]{2,1,0:T(8,128)(2,1)}, bf16[64,32,256]{2,1,0:T(8,128)(2,1)S(1)}, u32[]{:S(2)}, u32[]{:S(2)}) collective-permute-start(bf16[64,32,256]{2,1,0:T(8,128)(2,1)} %constant_dynamic-update-slice_fusion.12.mine_ref), channel_id=1, source_target_pairs={{0,16},{16,0},{1,17},{17,1},{2,18},{18,2},{3,19},{19,3},{4,20},{20... | collective-permute-start | bytes 3145736 | tf_op jit(solution)/shard_map/ppermute | solution.py:361

commit v4 on v2

--- a/solution.py
+++ b/solution.py
@@ -131,7 +131,7 @@
             pltpu.VMEM((3, TOK + half, WIN_LANES), jnp.bfloat16),
             pltpu.VMEM((TOK, WIN_LANES), jnp.bfloat16),
         ],
-        compiler_params=pltpu.CompilerParams(vmem_limit_bytes=24 * 2**20),
+        compiler_params=pltpu.CompilerParams(vmem_limit_bytes=14 * 2**20),
         name="window_attention",
     )(offset, own, below)
 
@@ -157,7 +157,7 @@
         tile_kernel,
         out_shape=jax.ShapeDtypeStruct((TOK, SW), jnp.bfloat16),
         scratch_shapes=[pltpu.VMEM((TOK, SW), jnp.bfloat16)],
-        compiler_params=pltpu.CompilerParams(vmem_limit_bytes=16 * 2**20),
+        compiler_params=pltpu.CompilerParams(vmem_limit_bytes=12 * 2**20),
         name="tile_attention",
     )(own)
 
@@ -180,10 +180,19 @@
 
 def project_kernel(
     place_ref, own_ref, left_ref, right_ref, far_a_ref, far_b_ref, shard_ref, mine_ref, other_ref,
-    out_ref, weights, sems,
+    out_ref, tokens, weights, sems,
 ):
     core, y, zh = place_ref[0], place_ref[1], place_ref[2]
     copies = []
+    row = 0
+    for src in (own_ref, left_ref, right_ref, far_a_ref, far_b_ref):
+        copies.append(
+            pltpu.make_async_copy(
+                src, tokens.at[pl.ds(row, src.shape[0]), :], sems.at[len(copies)]
+            )
+        )
+        copies[-1].start()
+        row += src.shape[0]
 
     def fetch(src, piece, part):
         rows = pl.ds(pl.multiple_of(part * SHARD, SHARD), SHARD)
@@ -203,9 +212,6 @@
                     lax.rem(zh + dz + 4, 4),
                 )
     weights[:, CHUNK:, :] = jnp.zeros((PIECES, CHUNK_PAD - CHUNK, PIECE), jnp.bfloat16)
-    tokens = jnp.concatenate(
-        [own_ref[...], left_ref[...], right_ref[...], far_a_ref[...], far_b_ref[...]], axis=0
-    )
     for copy in copies:
         copy.wait()
     for n in range(CHUNK_PAD // N_BLOCK):
@@ -213,7 +219,7 @@
         part = [weights[j, rows, :] for j in range(PIECES - 1)]
         part.append(weights[PIECES - 1, rows, 2 * LANES :])
         result = lax.dot_general(
-            tokens,
+            tokens[...],
             jnp.concatenate(part, axis=1),
             (((1,), (1,)), ((), ())),
             preferred_element_type=jnp.float32,
@@ -225,17 +231,19 @@
 
 def project(place, tokens, shard, mine, other):
     vmem = pl.BlockSpec(memory_space=pltpu.VMEM)
-    hbm = pl.BlockSpec(memory_space=pl.ANY)
+    hbm = pl.BlockSpec(memory_space=pltpu.HBM)
+    anywhere = pl.BlockSpec(memory_space=pl.ANY)
     return pl.pallas_call(
         project_kernel,
-        in_specs=[pl.BlockSpec(memory_space=pltpu.SMEM)] + [vmem] * 5 + [hbm] * 3,
+        in_specs=[pl.BlockSpec(memory_space=pltpu.SMEM)] + [hbm] * 5 + [anywhere] * 3,
         out_specs=vmem,
         out_shape=jax.ShapeDtypeStruct((COLS, XS * ROWS, CHUNK_PAD), jnp.bfloat16),
         scratch_shapes=[
+            pltpu.VMEM((XS * TOK, HRW), jnp.bfloat16),
             pltpu.VMEM((PIECES, CHUNK_PAD, PIECE), jnp.bfloat16),
-            pltpu.SemaphoreType.DMA((PIECES + 24,)),
-        ],
-        compiler_params=pltpu.CompilerParams(vmem_limit_bytes=40 * 2**20),
+            pltpu.SemaphoreType.DMA((PIECES + 24 + 5,)),
+        ],
+        compiler_params=pltpu.CompilerParams(vmem_limit_bytes=20 * 2**20),
         name="project",
     )(place, *tokens, shard, mine, other)
 
@@ -276,7 +284,7 @@
         + [pl.BlockSpec(memory_space=pltpu.VMEM)] * 6,
         out_shape=jax.ShapeDtypeStruct((TOK, SW), jnp.bfloat16),
         scratch_shapes=[pltpu.VMEM((PIECES, SW, LANES), jnp.bfloat16)],
-        compiler_params=pltpu.CompilerParams(vmem_limit_bytes=16 * 2**20),
+        compiler_params=pltpu.CompilerParams(vmem_limit_bytes=12 * 2**20),
         name="s_project",
     )(place, tokens, *raw)
 
@@ -348,7 +356,7 @@
         merge_kernel,
         out_shape=jax.ShapeDtypeStruct((TOK, F), jnp.bfloat16),
         scratch_shapes=[pltpu.VMEM((GROUPS, TOK, LANES), jnp.float32)],
-        compiler_params=pltpu.CompilerParams(vmem_limit_bytes=40 * 2**20),
+        compiler_params=pltpu.CompilerParams(vmem_limit_bytes=16 * 2**20),
         name="merge",
     )(
         hr, s_out, valid, padded(embed), embed[:, HRW:], padded(gain), gain[:, HRW:]
@@ -394,9 +402,9 @@
     near = neighbours(piece, "zh")
 
     tile_out = tile_attention(s_qkv.reshape(3, TOK, SW))
-    below = after(below, tile_out, near)
+    below = after(below, tile_out)
     window_out, passed = window_attention(shifts, own, below)
-    above = ring(passed, SPACE, 1)
+    above = ring(after(passed, near), SPACE, 1)
     near = after(near, window_out)
     foreign = jnp.concatenate(near + opposite(near, "zh"), axis=0)
 
@@ -404,15 +412,19 @@
     top = window_out[:, :MARGIN] + above.reshape(COLS, MARGIN, HRW)
     window_out = jnp.concatenate([top, window_out[:, MARGIN:]], axis=1).reshape(TOK, HRW)
     beside = neighbours(window_out, "x")
+    s_tokens = lax.all_to_all(
+        after(tile_out, foreign).reshape(COLS, ROWS, SW),
+        DATE,
+        split_axis=0,
+        concat_axis=0,
+        tiled=True,
+    )
     near = after(neighbours(foreign, "y"), beside)
     far = opposite(beside, "x")
     mine = jnp.concatenate((foreign,) + near + opposite(near, "y"), axis=0)
-    mine = after(mine, far)
+    mine = after(mine, far, s_tokens)
     other = ring(mine, "core", 1)
 
-    s_tokens = lax.all_to_all(
-        tile_out.reshape(COLS, ROWS, SW), DATE, split_axis=0, concat_axis=0, tiled=True
-    )
     hr_out = project(place, (window_out,) + beside + far, shard, mine, other)
     hr_out = lax.all_to_all(hr_out, DATE, split_axis=0, concat_axis=0, tiled=True)
 

time: 192 us -> 190 us (0.990)
  the two profiles are of different devices: /device:TPU:41 before, /device:TPU:96 now
where the time goes in v4:
time: 190 us; the launch traced here: 189 us
  starting transfers between devices  97.7 us (51%)
  waiting for transfers between devices  46.1 us (24%)
  local copies, waits for them, and re-layouts  23.4 us (12%)
  Pallas kernels  18 us (9%)
  other arithmetic  2.17 us (1%)
    ppermute x19, starting transfers between devices, ring(): return lax.ppermute(x, axis, [(i, (i + by) % size) for i in range(size)])  71.7 us
    ppermute x19, waiting for transfers between devices, ring(): return lax.ppermute(x, axis, [(i, (i + by) % size) for i in range(size)])  43.8 us
    all_to_all x1, starting transfers between devices, per_device(): lax.all_to_all(hr_out, DATE, split_axis=0, concat_axis=0, tiled=True)  14.2 us
    all_to_all x1, starting transfers between devices, per_device(): lax.all_to_all(after(tile_out, foreign).reshape(COLS, ROWS, SW), DATE, sp...  11.8 us
    unnamed x35, local copies, waits for them, and re-layouts  10.5 us
    pallas_call x1, Pallas kernels, project(): pl.pallas_call(project_kernel, in_specs=[pl.BlockSpec(memory_space=pltpu....  8.46 us
    slice x8, local copies, waits for them, and re-layouts, opposite(): return (ring(pair[0][:half], axis, 1), ring(pair[1][half:], axis, -1))  4.58 us
  transfers between devices with their start and end apart: 21, of which 9 were waited for; matrix products, arithmetic and copies ran while one was open for 9% of the time, Pallas kernels for 3%

profile of v4, /device:TPU:96, one launch (start us, length us, event | category | flops | bytes accessed | tf_op | source)
XLA Modules:
  0.0 188.5 jit_solution(8189408706294573102)
XLA Ops:
  0.0 2.4 %slice.68 = bf16[3,64,2816]{2,1,0:T(8,128)(2,1)} slice(bf16[3,128,2816]{2,1,0:T(8,128)(2,1)} %bitcast.34), slice={[0:3], [0:64], [0:2816]} | slice | bytes 2162688 | tf_op jit(solution)/shard_map/slice | solution.py:389
  2.4 1.9 %collective-permute-start = (bf16[3,64,2816]{2,1,0:T(8,128)(2,1)}, bf16[3,64,2816]{2,1,0:T(8,128)(2,1)S(1)}, u32[]{:S(2)}, u32[]{:S(2)}) collective-permute-start(bf16[3,64,2816]{2,1,0:T(8,128)(2,1)} %slice.68), channel_id=1, source_target_pairs={{0,496},{16,0},{32,16},{48,32},{64,48},{80,64},{96,80},{112,96},{1... | collective-permute-start | bytes 3244040 | tf_op jit(solution)/shard_map/ppermute | solution.py:368
  4.4 0.9 copy.15
  5.3 0.8 copy.19
  6.1 1.0 reshape.58
  7.1 1.0 dynamic-slice_bitcast_fusion
  8.2 10.5 %collective-permute-start.2 = (bf16[208,384]{1,0:T(8,128)(2,1)S(1)}, bf16[208,384]{1,0:T(8,128)(2,1)S(1)}, u32[]{:S(2)}, u32[]{:S(2)}) collective-permute-start(bf16[208,384]{1,0:T(8,128)(2,1)S(1)} %fusion.1), channel_id=1, source_target_pairs={{0,3},{1,0},{2,1},{3,2},{4,7},{5,4},{6,5},{7,6},{8,11},{9,8},{10,9... | collective-permute-start | bytes 479240 | tf_op jit(solution)/shard_map/ppermute | solution.py:368
  18.7 1.9 %collective-permute-start.1 = (bf16[208,384]{1,0:T(8,128)(2,1)S(1)}, bf16[208,384]{1,0:T(8,128)(2,1)S(1)}, u32[]{:S(2)}, u32[]{:S(2)}) collective-permute-start(bf16[208,384]{1,0:T(8,128)(2,1)S(1)} %fusion.1), channel_id=1, source_target_pairs={{0,1},{1,2},{2,3},{3,0},{4,5},{5,6},{6,7},{7,4},{8,9},{9,10},{10,1... | collective-permute-start | bytes 479240 | tf_op jit(solution)/shard_map/ppermute | solution.py:368
  21.2 1.1 copy-done.5
  22.4 0.8 tile_attention.1
  23.2 0.7 copy-done.2
  23.9 0.7 collective-permute-done.below_ref
  24.6 3.7 %window_attention.1 = (bf16[128,2816]{1,0:T(8,128)(2,1)S(1)}, bf16[64,2816]{1,0:T(8,128)(2,1)S(1)}) custom-call(s32[1]{0:T(128)S(6)} %copy.30.offset_ref, bf16[3,128,2816]{2,1,0:T(8,128)(2,1)S(1)} %bitcast.35, bf16[3,64,2816]{2,1,0:T(8,128)(2,1)S(1)} %collective-permute-done.below_ref), custom_call_target="tpu_custom_call" | custom-call | tf_op jit(solution)/shard_map/window_attention/pallas_call | solution.py:114
  28.4 6.9 %collective-permute-done.2 = bf16[208,384]{1,0:T(8,128)(2,1)S(1)} collective-permute-done((bf16[208,384]{1,0:T(8,128)(2,1)S(1)}, bf16[208,384]{1,0:T(8,128)(2,1)S(1)}, u32[]{:S(2)}, u32[]{:S(2)}) %collective-permute-start.2) | collective-permute-done | bytes 159776 | tf_op jit(solution)/shard_map/ppermute | solution.py:368
  35.3 1.9 %collective-permute-start.3 = (bf16[64,2816]{1,0:T(8,128)(2,1)S(1)}, bf16[64,2816]{1,0:T(8,128)(2,1)S(1)}, u32[]{:S(2)}, u32[]{:S(2)}) collective-permute-start(bf16[64,2816]{1,0:T(8,128)(2,1)S(1)} %get-tuple-element.18), channel_id=1, source_target_pairs={{0,16},{16,32},{32,48},{48,64},{64,80},{80,96},{96,112},{112,128},... | collective-permute-start | bytes 1081352 | tf_op jit(solution)/shard_map/ppermute | solution.py:368
  37.2 0.6 slice.56
  37.8 0.6 slice.57
  38.5 8.2 %collective-permute-start.9 = (bf16[104,384]{1,0:T(8,128)(2,1)}, bf16[104,384]{1,0:T(8,128)(2,1)}, u32[]{:S(2)}, u32[]{:S(2)}) collective-permute-start(bf16[104,384]{1,0:T(8,128)(2,1)} %slice.57), channel_id=1, source_target_pairs={{0,3},{1,0},{2,1},{3,2},{4,7},{5,4},{6,5},{7,6},{8,11},{9,8},{10,9... | collective-permute-start | bytes 239624 | tf_op jit(solution)/shard_map/ppermute | solution.py:368
  46.7 3.8 %collective-permute-start.8 = (bf16[104,384]{1,0:T(8,128)(2,1)}, bf16[104,384]{1,0:T(8,128)(2,1)}, u32[]{:S(2)}, u32[]{:S(2)}) collective-permute-start(bf16[104,384]{1,0:T(8,128)(2,1)} %slice.56), channel_id=1, source_target_pairs={{0,1},{1,2},{2,3},{3,0},{4,5},{5,6},{6,7},{7,4},{8,9},{9,10},{10,1... | collective-permute-start | bytes 239624 | tf_op jit(solution)/shard_map/ppermute | solution.py:368
  50.5 0.7 constant_dynamic-update-slice_fusion.3
  51.2 0.7 constant_dynamic-update-slice_fusion.2
  51.9 0.1 reshape.59
  52.0 1.7 slice_add_fusion
  53.7 0.4 maximum_bitcast_fusion.own_ref
  54.0 4.7 %collective-permute-start.5 = (bf16[128,2816]{1,0:T(8,128)(2,1)S(1)}, bf16[128,2816]{1,0:T(8,128)(2,1)S(1)}, u32[]{:S(2)}, u32[]{:S(2)}) collective-permute-start(bf16[128,2816]{1,0:T(8,128)(2,1)S(1)} %maximum_bitcast_fusion.own_ref), channel_id=1, source_target_pairs={{0,12},{4,0},{8,4},{12,8},{1,13},{5,1},{9,5},{13,9},{2,14},{6,2},{... | collective-permute-start | bytes 2162696 | tf_op jit(solution)/shard_map/ppermute | solution.py:368
  58.7 1.9 %collective-permute-start.4 = (bf16[128,2816]{1,0:T(8,128)(2,1)S(1)}, bf16[128,2816]{1,0:T(8,128)(2,1)}, u32[]{:S(2)}, u32[]{:S(2)}) collective-permute-start(bf16[128,2816]{1,0:T(8,128)(2,1)S(1)} %maximum_bitcast_fusion.own_ref), channel_id=1, source_target_pairs={{0,4},{4,8},{8,12},{12,0},{1,5},{5,9},{9,13},{13,1},{2,6},{6,10},{... | collective-permute-start | bytes 2162696 | tf_op jit(solution)/shard_map/ppermute | solution.py:368
  60.6 1.6 constant_dynamic-update-slice_fusion.1
  62.2 1.5 constant_dynamic-update-slice_fusion
  63.7 11.8 %all-to-all-start = ((bf16[16,8,1024]{2,1,0:T(8,128)(2,1)}), bf16[16,8,1024]{2,1,0:T(8,128)(2,1)}, u32[]{:S(2)}, u32[]{:S(2)}) async-start(bf16[16,8,1024]{2,1,0:T(8,128)(2,1)} %bitcast.38), calls=%async_computation | async-start | bytes 524288 | tf_op jit(solution)/shard_map/all_to_all | solution.py:415
  75.6 5.5 %collective-permute-start.11 = (bf16[624,384]{1,0:T(8,128)(2,1)}, bf16[624,384]{1,0:T(8,128)(2,1)S(1)}, u32[]{:S(2)}, u32[]{:S(2)}) collective-permute-start(bf16[624,384]{1,0:T(8,128)(2,1)} %get-tuple-element.31), channel_id=1, source_target_pairs={{0,384},{128,0},{256,128},{384,256},{1,385},{129,1},{257,129},{385... | collective-permute-start | bytes 1437704 | tf_op jit(solution)/shard_map/ppermute | solution.py:368
  81.1 1.9 %collective-permute-start.10 = (bf16[624,384]{1,0:T(8,128)(2,1)}, bf16[624,384]{1,0:T(8,128)(2,1)S(1)}, u32[]{:S(2)}, u32[]{:S(2)}) collective-permute-start(bf16[624,384]{1,0:T(8,128)(2,1)} %get-tuple-element.31), channel_id=1, source_target_pairs={{0,128},{128,256},{256,384},{384,0},{1,129},{129,257},{257,385},{3... | collective-permute-start | bytes 1437704 | tf_op jit(solution)/shard_map/ppermute | solution.py:368
  83.1 0.8 slice.72
  83.8 5.0 %collective-permute-start.7 = (bf16[64,2816]{1,0:T(8,128)(2,1)}, bf16[64,2816]{1,0:T(8,128)(2,1)}, u32[]{:S(2)}, u32[]{:S(2)}) collective-permute-start(bf16[64,2816]{1,0:T(8,128)(2,1)} %slice.72), channel_id=1, source_target_pairs={{0,12},{4,0},{8,4},{12,8},{1,13},{5,1},{9,5},{13,9},{2,14},{6,2},{... | collective-permute-start | bytes 1081352 | tf_op jit(solution)/shard_map/ppermute | solution.py:368
  88.8 1.7 slice.71
  90.6 1.9 %collective-permute-start.6 = (bf16[64,2816]{1,0:T(8,128)(2,1)}, bf16[64,2816]{1,0:T(8,128)(2,1)}, u32[]{:S(2)}, u32[]{:S(2)}) collective-permute-start(bf16[64,2816]{1,0:T(8,128)(2,1)} %slice.71), channel_id=1, source_target_pairs={{0,4},{4,8},{8,12},{12,0},{1,5},{5,9},{9,13},{13,1},{2,6},{6,10},{... | collective-permute-start | bytes 1081352 | tf_op jit(solution)/shard_map/ppermute | solution.py:368
  92.5 4.9 %collective-permute-done.10 = bf16[624,384]{1,0:T(8,128)(2,1)S(1)} collective-permute-done((bf16[624,384]{1,0:T(8,128)(2,1)}, bf16[624,384]{1,0:T(8,128)(2,1)S(1)}, u32[]{:S(2)}, u32[]{:S(2)}) %collective-permute-start.10) | collective-permute-done | bytes 479264 | tf_op jit(solution)/shard_map/ppermute | solution.py:368
  97.5 1.9 %collective-permute-start.13 = (bf16[312,384]{1,0:T(8,128)(2,1)S(1)}, bf16[312,384]{1,0:T(8,128)(2,1)S(1)}, u32[]{:S(2)}, u32[]{:S(2)}) collective-permute-start(bf16[312,384]{1,0:T(8,128)(2,1)S(1)} %slice.59), channel_id=1, source_target_pairs={{0,384},{128,0},{256,128},{384,256},{1,385},{129,1},{257,129},{385... | collective-permute-start | bytes 718856 | tf_op jit(solution)/shard_map/ppermute | solution.py:368
  99.4 3.9 %collective-permute-start.12 = (bf16[312,384]{1,0:T(8,128)(2,1)S(1)}, bf16[312,384]{1,0:T(8,128)(2,1)S(1)}, u32[]{:S(2)}, u32[]{:S(2)}) collective-permute-start(bf16[312,384]{1,0:T(8,128)(2,1)S(1)} %slice.58), channel_id=1, source_target_pairs={{0,128},{128,256},{256,384},{384,0},{1,129},{129,257},{257,385},{3... | collective-permute-start | bytes 718856 | tf_op jit(solution)/shard_map/ppermute | solution.py:368
  103.4 0.1 constant_dynamic-update-slice_fusion.6
  103.5 7.6 %collective-permute-done.12 = bf16[312,384]{1,0:T(8,128)(2,1)S(1)} collective-permute-done((bf16[312,384]{1,0:T(8,128)(2,1)S(1)}, bf16[312,384]{1,0:T(8,128)(2,1)S(1)}, u32[]{:S(2)}, u32[]{:S(2)}) %collective-permute-start.12) | collective-permute-done | bytes 239648 | tf_op jit(solution)/shard_map/ppermute | solution.py:368
  111.3 2.0 %collective-permute-start.14 = (bf16[2496,384]{1,0:T(8,128)(2,1)S(1)}, bf16[2496,384]{1,0:T(8,128)(2,1)}, u32[]{:S(2)}, u32[]{:S(2)}) collective-permute-start(bf16[2496,384]{1,0:T(8,128)(2,1)S(1)} %constant_dynamic-update-slice_fusion.4.mine_ref), channel_id=1, source_target_pairs={{0,16},{16,0},{1,17},{17,1},{2,18},{18,2},{3,19},{19,3},{4,20},{20... | collective-permute-start | bytes 5750792 | tf_op jit(solution)/shard_map/ppermute | solution.py:368
  113.4 3.8 %collective-permute-done.14.other_ref = bf16[2496,384]{1,0:T(8,128)(2,1)} collective-permute-done((bf16[2496,384]{1,0:T(8,128)(2,1)S(1)}, bf16[2496,384]{1,0:T(8,128)(2,1)}, u32[]{:S(2)}, u32[]{:S(2)}) %collective-permute-start.14) | collective-permute-done | bytes 1916960 | tf_op jit(solution)/shard_map/ppermute | solution.py:368
  117.2 1.2 copy-done.1
  118.4 8.5 %project.1 = bf16[16,32,768]{2,1,0:T(8,128)(2,1)} custom-call(s32[4]{0:T(128)S(1)} %pad_add_fusion.place_ref, bf16[128,2816]{1,0:T(8,128)(2,1)S(1)} %maximum_bitcast_fusion.own_ref, bf16[128,2816]{1,0:T(8,128)(2,1)} %collective-permute-done.4.left_ref, bf16[128,2816]{1,0:T(8,128)(2,1)S(1)} %collective-permute-done.5.right_ref, ...), custom_call_target="tpu_custom_call" | custom-call | tf_op jit(solution)/shard_map/project/pallas_call | solution.py:236
  126.9 14.2 %all-to-all-start.1 = ((bf16[16,32,768]{2,1,0:T(8,128)(2,1)}), bf16[16,32,768]{2,1,0:T(8,128)(2,1)S(1)}, u32[]{:S(2)}, u32[]{:S(2)}) async-start(bf16[16,32,768]{2,1,0:T(8,128)(2,1)} %project.1), calls=%async_computation.1 | async-start | bytes 1572864 | tf_op jit(solution)/shard_map/all_to_all | solution.py:429
  141.1 1.0 slice.74
  142.2 5.0 %collective-permute-start.16 = (bf16[32,32,256]{2,1,0:T(8,128)(2,1)S(1)}, bf16[32,32,256]{2,1,0:T(8,128)(2,1)S(1)}, u32[]{:S(2)}, u32[]{:S(2)}) collective-permute-start(bf16[32,32,256]{2,1,0:T(8,128)(2,1)S(1)} %pad_maximum_fusion.own_ref), channel_id=1, source_target_pairs={{0,12},{4,0},{8,4},{12,8},{1,13},{5,1},{9,5},{13,9},{2,14},{6,2},{... | collective-permute-start | bytes 1572872 | tf_op jit(solution)/shard_map/ppermute | solution.py:368
  147.2 1.9 %collective-permute-start.15 = (bf16[32,32,256]{2,1,0:T(8,128)(2,1)S(1)}, bf16[32,32,256]{2,1,0:T(8,128)(2,1)S(1)}, u32[]{:S(2)}, u32[]{:S(2)}) collective-permute-start(bf16[32,32,256]{2,1,0:T(8,128)(2,1)S(1)} %pad_maximum_fusion.own_ref), channel_id=1, source_target_pairs={{0,4},{4,8},{8,12},{12,0},{1,5},{5,9},{9,13},{13,1},{2,6},{6,10},{... | collective-permute-start | bytes 1572872 | tf_op jit(solution)/shard_map/ppermute | solution.py:368
  149.1 9.8 %collective-permute-done.16.right_ref = bf16[32,32,256]{2,1,0:T(8,128)(2,1)S(1)} collective-permute-done((bf16[32,32,256]{2,1,0:T(8,128)(2,1)S(1)}, bf16[32,32,256]{2,1,0:T(8,128)(2,1)S(1)}, u32[]{:S(2)}, u32[]{:S(2)}) %collective-permute-start.16) | collective-permute-done | bytes 524320 | tf_op jit(solution)/shard_map/ppermute | solution.py:368
  159.0 5.6 %collective-permute-start.18 = (bf16[16,32,256]{2,1,0:T(8,128)(2,1)S(1)}, bf16[16,32,256]{2,1,0:T(8,128)(2,1)S(1)}, u32[]{:S(2)}, u32[]{:S(2)}) collective-permute-start(bf16[16,32,256]{2,1,0:T(8,128)(2,1)S(1)} %slice.76), channel_id=1, source_target_pairs={{0,12},{4,0},{8,4},{12,8},{1,13},{5,1},{9,5},{13,9},{2,14},{6,2},{... | collective-permute-start | bytes 786440 | tf_op jit(solution)/shard_map/ppermute | solution.py:368
  164.6 0.7 slice.75
  165.3 2.1 %collective-permute-start.17 = (bf16[16,32,256]{2,1,0:T(8,128)(2,1)}, bf16[16,32,256]{2,1,0:T(8,128)(2,1)S(1)}, u32[]{:S(2)}, u32[]{:S(2)}) collective-permute-start(bf16[16,32,256]{2,1,0:T(8,128)(2,1)} %slice.75), channel_id=1, source_target_pairs={{0,4},{4,8},{8,12},{12,0},{1,5},{5,9},{9,13},{13,1},{2,6},{6,10},{... | collective-permute-start | bytes 786440 | tf_op jit(solution)/shard_map/ppermute | solution.py:368
  167.6 0.1 reshape.65.valid_ref
  167.7 0.1 reshape.69
  167.8 0.1 reshape.66
  168.1 1.2 collective-permute-done.18.far_b_ref
  169.3 0.7 copy-done.7
  170.0 8.7 %collective-permute-done.17.far_a_ref = bf16[16,32,256]{2,1,0:T(8,128)(2,1)S(1)} collective-permute-done((bf16[16,32,256]{2,1,0:T(8,128)(2,1)}, bf16[16,32,256]{2,1,0:T(8,128)(2,1)S(1)}, u32[]{:S(2)}, u32[]{:S(2)}) %collective-permute-start.17) | collective-permute-done | bytes 262176 | tf_op jit(solution)/shard_map/ppermute | solution.py:368
  178.7 0.9 copy-done.8
  179.6 1.7 s_project.1.s_ref
  181.4 0.7 copy-done.3
  182.1 2.3 %all-to-all-done.1.hr_ref = bf16[16,32,768]{2,1,0:T(8,128)(2,1)S(1)} async-done(((bf16[16,32,768]{2,1,0:T(8,128)(2,1)}), bf16[16,32,768]{2,1,0:T(8,128)(2,1)S(1)}, u32[]{:S(2)}, u32[]{:S(2)}) %all-to-all-start.1) | async-done | bytes 786464 | tf_op jit(solution)/shard_map/all_to_all | solution.py:429
  184.4 0.9 copy-done.4
  185.3 3.2 %merge.1 = bf16[128,3840]{1,0:T(8,128)(2,1)} custom-call(bf16[16,32,768]{2,1,0:T(8,128)(2,1)S(1)} %all-to-all-done.1.hr_ref, bf16[128,1024]{1,0:T(8,128)(2,1)S(1)} %copy-done.4, s32[1,128]{1,0:T(1,128)S(1)} %reshape.65.valid_ref, bf16[16,3072]{1,0:T(8,128)(2,1)S(1)} %bitcast.41, bf16[16,1024]{1,0:T(8,128)(2,1)S(1)} %slice.65.s_embed_ref, ...), custom_call_target="tpu_custom_call" | custom-call | tf_op jit(solution)/shard_map/merge/pallas_call | solution.py:355
  (50 shorter events, 0.7 us)
Async XLA Ops:
  0.0 24.6 %copy-start = (bf16[3,1,8,16,2816]{4,3,2,1,0:T(8,128)(2,1)S(1)}, bf16[3,1,8,16,2816]{4,3,2,1,0:T(8,128)(2,1)}, u32[]{:S(2)}) copy-start(bf16[3,1,8,16,2816]{4,3,2,1,0:T(8,128)(2,1)} %param.8) | copy-start | bytes 6488068
  2.4 22.2 %collective-permute-start = (bf16[3,64,2816]{2,1,0:T(8,128)(2,1)}, bf16[3,64,2816]{2,1,0:T(8,128)(2,1)S(1)}, u32[]{:S(2)}, u32[]{:S(2)}) collective-permute-start(bf16[3,64,2816]{2,1,0:T(8,128)(2,1)} %slice.68), channel_id=1, source_target_pairs={{0,496},{16,0},{32,16},{48,32},{64,48},{80,64},{96,80},{112,96},{1... | collective-permute-start | bytes 3244040 | tf_op jit(solution)/shard_map/ppermute | solution.py:368
  8.2 27.1 %collective-permute-start.2 = (bf16[208,384]{1,0:T(8,128)(2,1)S(1)}, bf16[208,384]{1,0:T(8,128)(2,1)S(1)}, u32[]{:S(2)}, u32[]{:S(2)}) collective-permute-start(bf16[208,384]{1,0:T(8,128)(2,1)S(1)} %fusion.1), channel_id=1, source_target_pairs={{0,3},{1,0},{2,1},{3,2},{4,7},{5,4},{6,5},{7,6},{8,11},{9,8},{10,9... | collective-permute-start | bytes 479240 | tf_op jit(solution)/shard_map/ppermute | solution.py:368
  18.7 16.6 %collective-permute-start.1 = (bf16[208,384]{1,0:T(8,128)(2,1)S(1)}, bf16[208,384]{1,0:T(8,128)(2,1)S(1)}, u32[]{:S(2)}, u32[]{:S(2)}) collective-permute-start(bf16[208,384]{1,0:T(8,128)(2,1)S(1)} %fusion.1), channel_id=1, source_target_pairs={{0,1},{1,2},{2,3},{3,0},{4,5},{5,6},{6,7},{7,4},{8,9},{9,10},{10,1... | collective-permute-start | bytes 479240 | tf_op jit(solution)/shard_map/ppermute | solution.py:368
  21.2 1.1 copy-start.5
  23.2 0.7 copy-start.2
  28.4 23.5 %copy-start.6 = (bf16[128,2816]{1,0:T(8,128)(2,1)}, bf16[128,2816]{1,0:T(8,128)(2,1)S(1)}, u32[]{:S(2)}) copy-start(bf16[128,2816]{1,0:T(8,128)(2,1)S(1)} %get-tuple-element.16) | copy-start | bytes 2162692
  35.3 16.6 %collective-permute-start.3 = (bf16[64,2816]{1,0:T(8,128)(2,1)S(1)}, bf16[64,2816]{1,0:T(8,128)(2,1)S(1)}, u32[]{:S(2)}, u32[]{:S(2)}) collective-permute-start(bf16[64,2816]{1,0:T(8,128)(2,1)S(1)} %get-tuple-element.18), channel_id=1, source_target_pairs={{0,16},{16,32},{32,48},{48,64},{64,80},{80,96},{96,112},{112,128},... | collective-permute-start | bytes 1081352 | tf_op jit(solution)/shard_map/ppermute | solution.py:368
  38.5 23.7 %collective-permute-start.9 = (bf16[104,384]{1,0:T(8,128)(2,1)}, bf16[104,384]{1,0:T(8,128)(2,1)}, u32[]{:S(2)}, u32[]{:S(2)}) collective-permute-start(bf16[104,384]{1,0:T(8,128)(2,1)} %slice.57), channel_id=1, source_target_pairs={{0,3},{1,0},{2,1},{3,2},{4,7},{5,4},{6,5},{7,6},{8,11},{9,8},{10,9... | collective-permute-start | bytes 239624 | tf_op jit(solution)/shard_map/ppermute | solution.py:368
  46.7 13.9 %collective-permute-start.8 = (bf16[104,384]{1,0:T(8,128)(2,1)}, bf16[104,384]{1,0:T(8,128)(2,1)}, u32[]{:S(2)}, u32[]{:S(2)}) collective-permute-start(bf16[104,384]{1,0:T(8,128)(2,1)} %slice.56), channel_id=1, source_target_pairs={{0,1},{1,2},{2,3},{3,0},{4,5},{5,6},{6,7},{7,4},{8,9},{9,10},{10,1... | collective-permute-start | bytes 239624 | tf_op jit(solution)/shard_map/ppermute | solution.py:368
  54.0 29.0 %collective-permute-start.5 = (bf16[128,2816]{1,0:T(8,128)(2,1)S(1)}, bf16[128,2816]{1,0:T(8,128)(2,1)S(1)}, u32[]{:S(2)}, u32[]{:S(2)}) collective-permute-start(bf16[128,2816]{1,0:T(8,128)(2,1)S(1)} %maximum_bitcast_fusion.own_ref), channel_id=1, source_target_pairs={{0,12},{4,0},{8,4},{12,8},{1,13},{5,1},{9,5},{13,9},{2,14},{6,2},{... | collective-permute-start | bytes 2162696 | tf_op jit(solution)/shard_map/ppermute | solution.py:368
  58.7 30.1 %collective-permute-start.4 = (bf16[128,2816]{1,0:T(8,128)(2,1)S(1)}, bf16[128,2816]{1,0:T(8,128)(2,1)}, u32[]{:S(2)}, u32[]{:S(2)}) collective-permute-start(bf16[128,2816]{1,0:T(8,128)(2,1)S(1)} %maximum_bitcast_fusion.own_ref), channel_id=1, source_target_pairs={{0,4},{4,8},{8,12},{12,0},{1,5},{5,9},{9,13},{13,1},{2,6},{6,10},{... | collective-permute-start | bytes 2162696 | tf_op jit(solution)/shard_map/ppermute | solution.py:368
  63.7 47.5 %all-to-all-start = ((bf16[16,8,1024]{2,1,0:T(8,128)(2,1)}), bf16[16,8,1024]{2,1,0:T(8,128)(2,1)}, u32[]{:S(2)}, u32[]{:S(2)}) async-start(bf16[16,8,1024]{2,1,0:T(8,128)(2,1)} %bitcast.38), calls=%async_computation | async-start | bytes 524288 | tf_op jit(solution)/shard_map/all_to_all | solution.py:415
  75.6 16.9 %collective-permute-start.11 = (bf16[624,384]{1,0:T(8,128)(2,1)}, bf16[624,384]{1,0:T(8,128)(2,1)S(1)}, u32[]{:S(2)}, u32[]{:S(2)}) collective-permute-start(bf16[624,384]{1,0:T(8,128)(2,1)} %get-tuple-element.31), channel_id=1, source_target_pairs={{0,384},{128,0},{256,128},{384,256},{1,385},{129,1},{257,129},{385... | collective-permute-start | bytes 1437704 | tf_op jit(solution)/shard_map/ppermute | solution.py:368
  81.1 16.3 %collective-permute-start.10 = (bf16[624,384]{1,0:T(8,128)(2,1)}, bf16[624,384]{1,0:T(8,128)(2,1)S(1)}, u32[]{:S(2)}, u32[]{:S(2)}) collective-permute-start(bf16[624,384]{1,0:T(8,128)(2,1)} %get-tuple-element.31), channel_id=1, source_target_pairs={{0,128},{128,256},{256,384},{384,0},{1,129},{129,257},{257,385},{3... | collective-permute-start | bytes 1437704 | tf_op jit(solution)/shard_map/ppermute | solution.py:368
  83.8 27.4 %collective-permute-start.7 = (bf16[64,2816]{1,0:T(8,128)(2,1)}, bf16[64,2816]{1,0:T(8,128)(2,1)}, u32[]{:S(2)}, u32[]{:S(2)}) collective-permute-start(bf16[64,2816]{1,0:T(8,128)(2,1)} %slice.72), channel_id=1, source_target_pairs={{0,12},{4,0},{8,4},{12,8},{1,13},{5,1},{9,5},{13,9},{2,14},{6,2},{... | collective-permute-start | bytes 1081352 | tf_op jit(solution)/shard_map/ppermute | solution.py:368
  90.6 20.7 %collective-permute-start.6 = (bf16[64,2816]{1,0:T(8,128)(2,1)}, bf16[64,2816]{1,0:T(8,128)(2,1)}, u32[]{:S(2)}, u32[]{:S(2)}) collective-permute-start(bf16[64,2816]{1,0:T(8,128)(2,1)} %slice.71), channel_id=1, source_target_pairs={{0,4},{4,8},{8,12},{12,0},{1,5},{5,9},{9,13},{13,1},{2,6},{6,10},{... | collective-permute-start | bytes 1081352 | tf_op jit(solution)/shard_map/ppermute | solution.py:368
  97.5 13.7 %collective-permute-start.13 = (bf16[312,384]{1,0:T(8,128)(2,1)S(1)}, bf16[312,384]{1,0:T(8,128)(2,1)S(1)}, u32[]{:S(2)}, u32[]{:S(2)}) collective-permute-start(bf16[312,384]{1,0:T(8,128)(2,1)S(1)} %slice.59), channel_id=1, source_target_pairs={{0,384},{128,0},{256,128},{384,256},{1,385},{129,1},{257,129},{385... | collective-permute-start | bytes 718856 | tf_op jit(solution)/shard_map/ppermute | solution.py:368
  99.4 11.7 %collective-permute-start.12 = (bf16[312,384]{1,0:T(8,128)(2,1)S(1)}, bf16[312,384]{1,0:T(8,128)(2,1)S(1)}, u32[]{:S(2)}, u32[]{:S(2)}) collective-permute-start(bf16[312,384]{1,0:T(8,128)(2,1)S(1)} %slice.58), channel_id=1, source_target_pairs={{0,128},{128,256},{256,384},{384,0},{1,129},{129,257},{257,385},{3... | collective-permute-start | bytes 718856 | tf_op jit(solution)/shard_map/ppermute | solution.py:368
  111.3 5.9 %collective-permute-start.14 = (bf16[2496,384]{1,0:T(8,128)(2,1)S(1)}, bf16[2496,384]{1,0:T(8,128)(2,1)}, u32[]{:S(2)}, u32[]{:S(2)}) collective-permute-start(bf16[2496,384]{1,0:T(8,128)(2,1)S(1)} %constant_dynamic-update-slice_fusion.4.mine_ref), channel_id=1, source_target_pairs={{0,16},{16,0},{1,17},{17,1},{2,18},{18,2},{3,19},{19,3},{4,20},{20... | collective-permute-start | bytes 5750792 | tf_op jit(solution)/shard_map/ppermute | solution.py:368
  117.2 1.2 copy-start.1
  126.9 57.5 %all-to-all-start.1 = ((bf16[16,32,768]{2,1,0:T(8,128)(2,1)}), bf16[16,32,768]{2,1,0:T(8,128)(2,1)S(1)}, u32[]{:S(2)}, u32[]{:S(2)}) async-start(bf16[16,32,768]{2,1,0:T(8,128)(2,1)} %project.1), calls=%async_computation.1 | async-start | bytes 1572864 | tf_op jit(solution)/shard_map/all_to_all | solution.py:429
  141.0 26.4 %copy-start.9 = (bf16[16,3840]{1,0:T(8,128)(2,1)S(1)}, bf16[16,3840]{1,0:T(8,128)(2,1)}, u32[]{:S(2)}) copy-start(bf16[16,3840]{1,0:T(8,128)(2,1)} %param.14) | copy-start | bytes 368644
  141.1 26.4 %copy-start.11 = (s32[16,8,1]{0,2,1:T(1,128)S(1)}, s32[16,8,1]{0,2,1:T(1,128)}, u32[]{:S(2)}) copy-start(s32[16,8,1]{0,2,1:T(1,128)} %param.13) | copy-start | bytes 1540
  141.1 26.6 %copy-start.10 = (f32[3840]{0:T(1024)S(1)}, f32[3840]{0:T(1024)}, u32[]{:S(2)}) copy-start(f32[3840]{0:T(1024)} %param.15) | copy-start | bytes 46084
  142.2 16.8 %collective-permute-start.16 = (bf16[32,32,256]{2,1,0:T(8,128)(2,1)S(1)}, bf16[32,32,256]{2,1,0:T(8,128)(2,1)S(1)}, u32[]{:S(2)}, u32[]{:S(2)}) collective-permute-start(bf16[32,32,256]{2,1,0:T(8,128)(2,1)S(1)} %pad_maximum_fusion.own_ref), channel_id=1, source_target_pairs={{0,12},{4,0},{8,4},{12,8},{1,13},{5,1},{9,5},{13,9},{2,14},{6,2},{... | collective-permute-start | bytes 1572872 | tf_op jit(solution)/shard_map/ppermute | solution.py:368
  147.2 17.4 %collective-permute-start.15 = (bf16[32,32,256]{2,1,0:T(8,128)(2,1)S(1)}, bf16[32,32,256]{2,1,0:T(8,128)(2,1)S(1)}, u32[]{:S(2)}, u32[]{:S(2)}) collective-permute-start(bf16[32,32,256]{2,1,0:T(8,128)(2,1)S(1)} %pad_maximum_fusion.own_ref), channel_id=1, source_target_pairs={{0,4},{4,8},{8,12},{12,0},{1,5},{5,9},{9,13},{13,1},{2,6},{6,10},{... | collective-permute-start | bytes 1572872 | tf_op jit(solution)/shard_map/ppermute | solution.py:368
  159.0 10.3 %collective-permute-start.18 = (bf16[16,32,256]{2,1,0:T(8,128)(2,1)S(1)}, bf16[16,32,256]{2,1,0:T(8,128)(2,1)S(1)}, u32[]{:S(2)}, u32[]{:S(2)}) collective-permute-start(bf16[16,32,256]{2,1,0:T(8,128)(2,1)S(1)} %slice.76), channel_id=1, source_target_pairs={{0,12},{4,0},{8,4},{12,8},{1,13},{5,1},{9,5},{13,9},{2,14},{6,2},{... | collective-permute-start | bytes 786440 | tf_op jit(solution)/shard_map/ppermute | solution.py:368
  165.3 13.4 %collective-permute-start.17 = (bf16[16,32,256]{2,1,0:T(8,128)(2,1)}, bf16[16,32,256]{2,1,0:T(8,128)(2,1)S(1)}, u32[]{:S(2)}, u32[]{:S(2)}) collective-permute-start(bf16[16,32,256]{2,1,0:T(8,128)(2,1)} %slice.75), channel_id=1, source_target_pairs={{0,4},{4,8},{8,12},{12,0},{1,5},{5,9},{9,13},{13,1},{2,6},{6,10},{... | collective-permute-start | bytes 786440 | tf_op jit(solution)/shard_map/ppermute | solution.py:368
  169.3 0.7 copy-start.7
  178.7 1.0 copy-start.8
  181.4 0.7 copy-start.3
  184.4 1.0 copy-start.4
